TPU v7x, 32 devices: a whole 2x2x4 slice. The times are simulated.
32 devices in a mesh: rep: 4 (over z), exp: 8 (over y, x, core).
Axes of the slice: x: 2, y: 2, z: 4, core: 2. Of those that a mesh axis runs over, the one named last changes fastest.
Arguments:
- tokens: bfloat16 [36864, 768], P(('rep', 'exp')), may hold values from -6 to 6
- cotangent: bfloat16 [36864, 768], P(('rep', 'exp')), may hold values from -6 to 6
- expert_ids: int32 [36864, 2], P(('rep', 'exp')), may hold values from 0 to 7, as said below
- expert_slots: int32 [36864, 2], P(('rep', 'exp')), may hold values from -1 to 143, as said below
- w_qkv: bfloat16 [768, 2304], replicated, may hold values from -0.21875 to 0.21875
- q_bias: bfloat16 [768], replicated, may hold values from -1.75 to 1.75
- v_bias: bfloat16 [768], replicated, may hold values from -1.75 to 1.75
- w_proj: bfloat16 [768, 768], replicated, may hold values from -0.875 to 0.875
- proj_bias: bfloat16 [768], replicated, may hold values from -1.75 to 1.75
- gain_one: float32 [768], replicated, may hold values from 0.25 to 1.75
- shift_one: float32 [768], replicated, may hold values from -1.75 to 1.75
- gain_two: float32 [768], replicated, may hold values from 0.25 to 1.75
- shift_two: float32 [768], replicated, may hold values from -1.75 to 1.75
- w_router: float32 [768, 8], replicated, may hold values from -0.15625 to 0.15625
- expert_in: bfloat16 [8, 768, 3072], P('exp'), may hold values from -0.21875 to 0.21875
- expert_in_bias: bfloat16 [8, 3072], P('exp'), may hold values from -1.75 to 1.75
- expert_out: bfloat16 [8, 3072, 768], P('exp'), may hold values from -0.4375 to 0.4375
- expert_out_bias: bfloat16 [8, 768], P('exp'), may hold values from -1.5 to 1.5
Outputs:
- mixed: bfloat16 [36864, 768], P(('rep', 'exp'))
- grad_tokens: float32 [36864, 768], P(('rep', 'exp'))
- grad_w_qkv: float32 [768, 2304], replicated
- grad_q_bias: float32 [768], replicated
- grad_v_bias: float32 [768], replicated
- grad_w_proj: float32 [768, 768], replicated
- grad_proj_bias: float32 [768], replicated
- grad_gain_one: float32 [768], replicated
- grad_shift_one: float32 [768], replicated
- grad_gain_two: float32 [768], replicated
- grad_shift_two: float32 [768], replicated
- grad_w_router: float32 [768, 8], replicated
- grad_expert_in: float32 [8, 768, 3072], P('exp', None, 'rep')
- grad_expert_in_bias: float32 [8, 3072], P('exp', 'rep')
- grad_expert_out: float32 [8, 3072, 768], P('exp', 'rep')
- grad_expert_out_bias: float32 [8, 768], P('exp', 'rep')
Inputs may be any that keep to these rules, and one draw needn't show every extreme that they name: `expert_ids`: the two experts of a patch differ. `expert_slots`: among the pairs of one device (aligned blocks of 1152 rows), each expert's kept pairs hold the slots 0, 1, 2, ... once each in a priority order of those pairs, and a pair is -1 exactly when its expert already has 144 pairs of that device before it.
All inputs are finite; a program needn't handle non-finite values.
Results may differ from a plain program's by a relative error of at most 0.014.
Values may be sent and summed in bfloat16 or wider, within the bound.
No kernel may reach another device: no remote copies, remote signals or barrier semaphores. Data moves between devices by JAX's collectives and lax.ppermute only.
A program may use at most 192 MiB of HBM per device.

v0:
```python
import jax
import jax.numpy as jnp
from jax import lax
from jax.sharding import PartitionSpec as P

HEADS = 12
HEAD_DIM = 64
SEQ = 576


EPSILON = 1e-06
HIGHEST = lax.Precision.HIGHEST


def norm_forward(field, norm_gain, norm_shift):
    average = jnp.mean(field, axis=-1, keepdims=True)
    centred = field - average
    variance = jnp.mean(centred * centred, axis=-1, keepdims=True)
    inverse = lax.rsqrt(variance + EPSILON)
    unit_rows = centred * inverse
    return (unit_rows * norm_gain + norm_shift, unit_rows, inverse)


def norm_backward(grad_out, unit_rows, inverse, norm_gain):
    grad_unit = grad_out * norm_gain
    centred = grad_unit - jnp.mean(grad_unit, axis=-1, keepdims=True)
    along = unit_rows * jnp.mean(grad_unit * unit_rows, axis=-1, keepdims=True)
    return (
        inverse * (centred - along),
        jnp.sum(grad_out * unit_rows, axis=0),
        jnp.sum(grad_out, axis=0),
    )


def by_heads(block):
    return block.reshape(block.shape[0], HEADS, HEAD_DIM)


def contract_last(left, right):
    return lax.dot_general(
        left, right, (((1,), (1,)), ((), ())), preferred_element_type=jnp.float32
    )


def contract_first(left, right):
    return lax.dot_general(
        left, right, (((0,), (0,)), ((), ())), preferred_element_type=jnp.float32
    )


def contract_first_high(left, right):
    return lax.dot_general(
        left, right, (((0,), (0,)), ((), ())), precision=HIGHEST, preferred_element_type=jnp.float32
    )


def exact_gelu(field):
    return jax.nn.gelu(field, approximate=False)


def image_scores(queries, key_rows):
    return jnp.einsum(
        "qhd,khd->hqk", by_heads(queries), by_heads(key_rows), preferred_element_type=jnp.float32
    ) * HEAD_DIM ** (-0.5)


def attend_image(pieces):
    queries, key_rows, values = pieces
    scores = image_scores(queries, key_rows)
    row_max = jnp.max(scores, axis=-1, keepdims=True)
    exponent = jnp.exp(scores - row_max)
    row_total = jnp.sum(exponent, axis=-1, keepdims=True)
    weights = (exponent / row_total).astype(jnp.bfloat16)
    context = jnp.einsum(
        "hqk,khd->qhd", weights, by_heads(values), preferred_element_type=jnp.float32
    )
    return (context.reshape(queries.shape[0], -1), (row_max + jnp.log(row_total))[..., 0])


def attend_back(pieces):
    queries, key_rows, values, grad_context, log_total = pieces
    scores = image_scores(queries, key_rows)
    probs = jnp.exp(scores - log_total[..., None])
    weights = probs.astype(jnp.bfloat16)
    grad_heads = by_heads(grad_context)
    grad_probs = jnp.einsum(
        "qhd,khd->hqk", grad_heads, by_heads(values), preferred_element_type=jnp.float32
    )
    grad_values = jnp.einsum(
        "hqk,qhd->khd", weights, grad_heads, preferred_element_type=jnp.float32
    )
    grad_scores = (
        probs * (grad_probs - jnp.sum(probs * grad_probs, axis=-1, keepdims=True))
    ).astype(jnp.bfloat16)
    grad_queries = jnp.einsum(
        "hqk,khd->qhd", grad_scores, by_heads(key_rows), preferred_element_type=jnp.float32
    ) * HEAD_DIM ** (-0.5)
    grad_keys = jnp.einsum(
        "hqk,qhd->khd", grad_scores, by_heads(queries), preferred_element_type=jnp.float32
    ) * HEAD_DIM ** (-0.5)
    length = queries.shape[0]
    joined = jnp.concatenate(
        [
            grad_queries.reshape(length, -1),
            grad_keys.reshape(length, -1),
            grad_values.reshape(length, -1),
        ],
        axis=1,
    )
    return joined.astype(jnp.bfloat16)


def expert_backward(rows_in, grads_out, weight_in, bias_in, weight_out):
    hidden = jnp.dot(rows_in, weight_in, preferred_element_type=jnp.float32) + bias_in
    activated, gelu_back = jax.vjp(exact_gelu, hidden)
    grad_hidden = gelu_back(contract_last(grads_out, weight_out))[0].astype(jnp.bfloat16)
    return (activated.astype(jnp.bfloat16), grad_hidden)


def on_device(
    tokens,
    cotangent,
    expert_ids,
    expert_slots,
    w_qkv,
    q_bias,
    v_bias,
    w_proj,
    proj_bias,
    gain_one,
    shift_one,
    gain_two,
    shift_two,
    w_router,
    expert_in,
    expert_in_bias,
    expert_out,
    expert_out_bias,
):
    row_count, model_width = tokens.shape
    experts = w_router.shape[1]
    slot_count = row_count // experts
    images = row_count // SEQ
    inputs = tokens.astype(jnp.float32)
    normed_one, unit_one, inverse_one = norm_forward(inputs, gain_one, shift_one)
    normed_one = normed_one.astype(jnp.bfloat16)
    bias_row = jnp.concatenate(
        [
            q_bias.astype(jnp.float32),
            jnp.zeros((model_width,), jnp.float32),
            v_bias.astype(jnp.float32),
        ]
    )
    projected = (jnp.dot(normed_one, w_qkv, preferred_element_type=jnp.float32) + bias_row).astype(
        jnp.bfloat16
    )
    image_blocks = projected.reshape(images, SEQ, 3 * model_width)
    query_blocks = image_blocks[:, :, :model_width]
    key_blocks = image_blocks[:, :, model_width : 2 * model_width]
    value_blocks = image_blocks[:, :, 2 * model_width :]
    context, log_total = lax.map(attend_image, (query_blocks, key_blocks, value_blocks))
    context = context.reshape(row_count, model_width).astype(jnp.bfloat16)
    branch = jnp.dot(context, w_proj, preferred_element_type=jnp.float32) + proj_bias.astype(
        jnp.float32
    )
    residual = inputs + branch
    normed_two, unit_two, inverse_two = norm_forward(residual, gain_two, shift_two)
    normed_two = normed_two.astype(jnp.bfloat16)
    router = jax.nn.softmax(
        jnp.dot(normed_two.astype(jnp.float32), w_router, precision=HIGHEST), axis=-1
    )
    columns = jnp.where(expert_slots >= 0, expert_ids * slot_count + expert_slots, -1)
    target = lax.broadcasted_iota(jnp.int32, (1, experts * slot_count), 1)
    first_hit = (columns[:, 0:1] == target).astype(jnp.bfloat16)
    second_hit = (columns[:, 1:2] == target).astype(jnp.bfloat16)
    either = first_hit + second_hit
    hits = jnp.concatenate([first_hit, second_hit], axis=0)
    chosen = (expert_ids[:, :, None] == lax.broadcasted_iota(jnp.int32, (1, 1, experts), 2)).astype(
        jnp.float32
    )
    gate_values = jnp.sum(router[:, None, :] * chosen, axis=-1)
    outgoing = (
        contract_first(either, normed_two)
        .astype(jnp.bfloat16)
        .reshape(experts, slot_count, model_width)
    )
    arrived = lax.all_to_all(outgoing, "exp", split_axis=0, concat_axis=0, tiled=True).reshape(
        row_count, model_width
    )
    weight_in = expert_in[0]
    bias_in = expert_in_bias[0].astype(jnp.float32)
    weight_out = expert_out[0]
    bias_out = expert_out_bias[0].astype(jnp.float32)
    hidden = jnp.dot(arrived, weight_in, preferred_element_type=jnp.float32) + bias_in
    activated = exact_gelu(hidden).astype(jnp.bfloat16)
    produced = (
        jnp.dot(activated, weight_out, preferred_element_type=jnp.float32) + bias_out
    ).astype(jnp.bfloat16)
    returned = lax.all_to_all(
        produced.reshape(experts, slot_count, model_width),
        "exp",
        split_axis=0,
        concat_axis=0,
        tiled=True,
    ).reshape(row_count, model_width)
    picked_both = jnp.dot(hits, returned, preferred_element_type=jnp.float32)
    picked_first = picked_both[:row_count]
    picked_second = picked_both[row_count:]
    final = residual + gate_values[:, 0:1] * picked_first + gate_values[:, 1:2] * picked_second
    mixed = final.astype(jnp.bfloat16)
    grad_out = cotangent.astype(jnp.float32)
    grad_gates = jnp.stack(
        [jnp.sum(grad_out * picked_first, axis=-1), jnp.sum(grad_out * picked_second, axis=-1)],
        axis=-1,
    )
    grad_router = jnp.sum(grad_gates[:, :, None] * chosen, axis=1)
    grad_logits = router * (grad_router - jnp.sum(router * grad_router, axis=-1, keepdims=True))
    grad_picked = jnp.concatenate(
        [gate_values[:, 0:1] * grad_out, gate_values[:, 1:2] * grad_out], axis=0
    ).astype(jnp.bfloat16)
    grad_returned = (
        contract_first(hits, grad_picked)
        .astype(jnp.bfloat16)
        .reshape(experts, slot_count, model_width)
    )
    grad_produced = lax.all_to_all(
        grad_returned, "exp", split_axis=0, concat_axis=0, tiled=True
    ).reshape(row_count, model_width)
    act_round, grad_hidden = expert_backward(arrived, grad_produced, weight_in, bias_in, weight_out)
    grad_arrived = (
        contract_last(grad_hidden, weight_in)
        .astype(jnp.bfloat16)
        .reshape(experts, slot_count, model_width)
    )
    grad_source = lax.all_to_all(
        grad_arrived, "exp", split_axis=0, concat_axis=0, tiled=True
    ).reshape(row_count, model_width)
    local_in = contract_first(arrived, grad_hidden)[None]
    local_in_bias = jnp.sum(grad_hidden.astype(jnp.float32), axis=0)[None]
    local_out = contract_first(act_round, grad_produced)[None]
    local_out_bias = jnp.sum(grad_produced.astype(jnp.float32), axis=0)[None]
    grad_ein, grad_einb, grad_eout, grad_eoutb = (
        lax.psum_scatter(
            local_in.astype(jnp.bfloat16), "rep", scatter_dimension=2, tiled=True
        ).astype(jnp.float32),
        lax.psum_scatter(
            local_in_bias.astype(jnp.bfloat16), "rep", scatter_dimension=1, tiled=True
        ).astype(jnp.float32),
        lax.psum_scatter(
            local_out.astype(jnp.bfloat16), "rep", scatter_dimension=1, tiled=True
        ).astype(jnp.float32),
        lax.psum_scatter(
            local_out_bias.astype(jnp.bfloat16), "rep", scatter_dimension=1, tiled=True
        ).astype(jnp.float32),
    )
    grad_normed_two = jnp.dot(either, grad_source, preferred_element_type=jnp.float32)
    grad_normed_two = grad_normed_two + lax.dot_general(
        grad_logits,
        w_router,
        (((1,), (1,)), ((), ())),
        precision=HIGHEST,
        preferred_element_type=jnp.float32,
    )
    local_router = contract_first_high(normed_two.astype(jnp.float32), grad_logits)
    grad_from_norm, local_gain_two, local_shift_two = norm_backward(
        grad_normed_two, unit_two, inverse_two, gain_two
    )
    grad_residual = grad_out + grad_from_norm
    grad_branch = grad_residual.astype(jnp.bfloat16)
    local_proj = contract_first(context, grad_branch)
    local_proj_bias = jnp.sum(grad_branch.astype(jnp.float32), axis=0)
    grad_context = contract_last(grad_branch, w_proj).astype(jnp.bfloat16)
    grad_qkv = lax.map(
        attend_back,
        (
            query_blocks,
            key_blocks,
            value_blocks,
            grad_context.reshape(images, SEQ, model_width),
            log_total,
        ),
    )
    grad_qkv = grad_qkv.reshape(row_count, 3 * model_width)
    local_qkv = contract_first(normed_one, grad_qkv)
    grad_wide = grad_qkv.astype(jnp.float32)
    local_q_bias = jnp.sum(grad_wide[:, :model_width], axis=0)
    local_v_bias = jnp.sum(grad_wide[:, 2 * model_width :], axis=0)
    grad_normed_one = contract_last(grad_qkv, w_qkv)
    grad_from_first, local_gain_one, local_shift_one = norm_backward(
        grad_normed_one, unit_one, inverse_one, gain_one
    )
    grad_tokens = grad_residual + grad_from_first
    (
        grad_w_qkv,
        grad_q_bias,
        grad_v_bias,
        grad_w_proj,
        grad_proj_bias,
        grad_gain_one,
        grad_shift_one,
        grad_gain_two,
        grad_shift_two,
        grad_w_router,
    ) = lax.psum(
        (
            local_qkv,
            local_q_bias,
            local_v_bias,
            local_proj,
            local_proj_bias,
            local_gain_one,
            local_shift_one,
            local_gain_two,
            local_shift_two,
            local_router,
        ),
        ("rep", "exp"),
    )
    return (
        mixed,
        grad_tokens,
        grad_w_qkv,
        grad_q_bias,
        grad_v_bias,
        grad_w_proj,
        grad_proj_bias,
        grad_gain_one,
        grad_shift_one,
        grad_gain_two,
        grad_shift_two,
        grad_w_router,
        grad_ein,
        grad_einb,
        grad_eout,
        grad_eoutb,
    )


def solution(mesh):
    placed = (
        P(("rep", "exp"), None),
        P(("rep", "exp"), None),
        P(("rep", "exp"), None),
        P(("rep", "exp"), None),
        P(),
        P(),
        P(),
        P(),
        P(),
        P(),
        P(),
        P(),
        P(),
        P(),
        P("exp", None, None),
        P("exp", None),
        P("exp", None, None),
        P("exp", None),
    )
    return jax.shard_map(
        on_device,
        mesh=mesh,
        in_specs=placed,
        out_specs=(
            P(("rep", "exp"), None),
            P(("rep", "exp"), None),
            P(),
            P(),
            P(),
            P(),
            P(),
            P(),
            P(),
            P(),
            P(),
            P(),
            P("exp", None, "rep"),
            P("exp", "rep"),
            P("exp", "rep", None),
            P("exp", "rep"),
        ),
        check_vma=False,
    )
```

profile of v0, /device:TPU:0, one launch (start us, length us, event | category | flops | bytes accessed | tf_op | source)
XLA Modules:
  0.0 720.9 jit_solution(12045565676149617166)
XLA Ops:
  20.3 5.7 fusion.18
  40.2 76.1 %while.22 = (s32[]{:T(128)}, bf16[2,576,768]{2,1,0:T(8,128)(2,1)}, f32[2,12,576]{2,1,0:T(8,128)}, bf16[2,576,768]{1,2,0:T(8,128)(2,1)}, bf16[2,576,768]{1,2,0:T(...) while((s32[]{:T(128)}, bf16[2,576,768]{2,1,0:T(8,128)(2,1)}, f32[2,12,576]{2,1,0:T(8,128)}, ...), condition=%wide.region_5.6_spmd, body=%wide.region_2.5_spmd.sunk | while | flops 1055040768 | bytes 61086932 | solution.py:161
  44.4 8.1 %multiply_reduce_fusion.10 = (f32[12,576]{1,0:T(8,128)}, f32[12,576,576]{1,2,0:T(8,128)}) fusion(bf16[576,12,64]{0,2,1:T(8,128)(2,1)S(1)} %bitcast.162, bf16[576,12,64]{0,2,1:T(8,128)(2,1)S(1)} %bitcast.161), kind=kOutput, calls=%fused_computation.2.clone.1 | convolution fusion | flops 517563648 | bytes 17722368 | tf_op jit(solution)/shard_map/while/body/eval_jaxpr/qhd,khd->hqk/dot_general | solution.py:62
  52.4 9.7 %fusion.143 = f32[12,576]{1,0:T(8,128)} fusion(f32[12,576,576]{1,2,0:T(8,128)} %get-tuple-element.347, f32[12,576]{1,0:T(8,128)} %get-tuple-element.348), kind=kLoop, calls=%fused_computation.3.clone.1 | loop fusion | flops 11937024 | bytes 15980544 | tf_op jit(solution)/shard_map/while/body/eval_jaxpr/reduce_sum | solution.py:72
  62.1 11.1 %fusion.144 = bf16[12,64,576]{2,1,0:T(8,128)(2,1)} fusion(bf16[576,12,64]{0,2,1:T(8,128)(2,1)} %bitcast.167, f32[12,576,576]{1,2,0:T(8,128)} %get-tuple-element.347, f32[12,576]{1,0:T(8,128)} %fusion.143, f32[12,576]{1,0:T(8,128)} %get-tuple-element.348), kind=kOutput, calls=%fused_computation.4.clone.1 | convolution fusion | flops 525533184 | bytes 17750016 | tf_op jit(solution)/shard_map/while/body/eval_jaxpr/hqk,khd->qhd/dot_general | solution.py:74
  82.0 8.1 %multiply_reduce_fusion.10 = (f32[12,576]{1,0:T(8,128)}, f32[12,576,576]{1,2,0:T(8,128)}) fusion(bf16[576,12,64]{0,2,1:T(8,128)(2,1)S(1)} %bitcast.162, bf16[576,12,64]{0,2,1:T(8,128)(2,1)S(1)} %bitcast.161), kind=kOutput, calls=%fused_computation.2.clone.1 | convolution fusion | flops 517563648 | bytes 17722368 | tf_op jit(solution)/shard_map/while/body/eval_jaxpr/qhd,khd->hqk/dot_general | solution.py:62
  90.1 9.7 %fusion.143 = f32[12,576]{1,0:T(8,128)} fusion(f32[12,576,576]{1,2,0:T(8,128)} %get-tuple-element.347, f32[12,576]{1,0:T(8,128)} %get-tuple-element.348), kind=kLoop, calls=%fused_computation.3.clone.1 | loop fusion | flops 11937024 | bytes 15980544 | tf_op jit(solution)/shard_map/while/body/eval_jaxpr/reduce_sum | solution.py:72
  99.8 11.1 %fusion.144 = bf16[12,64,576]{2,1,0:T(8,128)(2,1)} fusion(bf16[576,12,64]{0,2,1:T(8,128)(2,1)} %bitcast.167, f32[12,576,576]{1,2,0:T(8,128)} %get-tuple-element.347, f32[12,576]{1,0:T(8,128)} %fusion.143, f32[12,576]{1,0:T(8,128)} %get-tuple-element.348), kind=kOutput, calls=%fused_computation.4.clone.1 | convolution fusion | flops 525533184 | bytes 17750016 | tf_op jit(solution)/shard_map/while/body/eval_jaxpr/hqk,khd->qhd/dot_general | solution.py:74
  141.2 14.5 %all-to-all-done = bf16[8,144,768]{2,1,0:T(8,128)(2,1)} async-done(((bf16[8,144,768]{2,1,0:T(8,128)(2,1)}), bf16[8,144,768]{2,1,0:T(8,128)(2,1)}, u32[]{:S(2)}, u32[]{:S(2)}) %all-to-all-start) | async-done | bytes 1769504 | tf_op jit(solution)/shard_map/all_to_all | solution.py:187
  155.7 40.7 %multiply_convert_fusion.3 = (bf16[1152,3072]{1,0:T(8,128)(2,1)S(1)}, f32[1152,3072]{1,0:T(8,128)}, f32[1152,3072]{1,0:T(8,128)}) fusion(f32[3072]{0:T(1024)S(1)} %bitcast.180, bf16[1152,768]{1,0:T(8,128)(2,1)} %bitcast.20, bf16[1,768,3072]{2,1,0:T(8,128)(2,1)} %param.36), kind=kOutput, calls=%fused_computation.32 | convolution fusion | flops 5669388288 | bytes 41889792 | tf_op jit(solution)/shard_map/dot_general | solution.py:194
  196.4 6.8 fusion.61
  213.1 17.7 %all-to-all-done.1 = bf16[8,144,768]{2,1,0:T(8,128)(2,1)} async-done(((bf16[8,144,768]{2,1,0:T(8,128)(2,1)}), bf16[8,144,768]{2,1,0:T(8,128)(2,1)}, u32[]{:S(2)}, u32[]{:S(2)}) %all-to-all-start.1) | async-done | bytes 1769504 | tf_op jit(solution)/shard_map/all_to_all | solution.py:199
  230.8 8.0 %fusion.54 = f32[2304,768]{0,1:T(8,128)S(1)} fusion(bf16[1152,768]{1,0:T(8,128)(2,1)} %bitcast.25, bf16[1152,1152]{1,0:T(8,128)(2,1)} %get-tuple-element.263, bf16[1152,1152]{1,0:T(8,128)(2,1)} %get-tuple-element.262), kind=kOutput, calls=%fused_computation.105 | convolution fusion | flops 4087480320 | bytes 14155776 | tf_op jit(solution)/shard_map/dot_general | solution.py:206
  248.6 26.2 %all_to_all.20 = bf16[8,144,768]{2,1,0:T(8,128)(2,1)} all-to-all(bf16[8,144,768]{2,1,0:T(8,128)(2,1)S(1)} %bitcast.177), channel_id=1, replica_groups=mesh['rep'=4,'exp'=8] {'exp'}, dimensions={0} | all-to-all | bytes 3538944 | tf_op jit(solution)/shard_map/all_to_all | solution.py:226
  278.8 20.9 %fusion.86 = (bf16[3072]{0:T(1024)(128)(2,1)}, bf16[1152,3072]{1,0:T(8,128)(2,1)}) fusion(f32[1152,3072]{1,0:T(8,128)} %get-tuple-element.237, f32[1152,3072]{1,0:T(8,128)} %get-tuple-element.254, bf16[1152,768]{1,0:T(8,128)(2,1)} %bitcast.169, bf16[1,3072,768]{2,1,0:T(8,128)(2,1)} %param.38), kind=kOutput, calls=%fused_computation.154 | convolution fusion | flops 5488899072 | bytes 41883648 | tf_op jit(solution)/shard_map/dot_general | solution.py:40
  301.8 10.6 %fusion.28 = bf16[1,3072,768]{2,1,0:T(8,128)(2,1)} fusion(bf16[1152,3072]{1,0:T(8,128)(2,1)} %copy-done.59, bf16[1152,768]{1,0:T(8,128)(2,1)} %bitcast.170), kind=kOutput, calls=%fused_computation.71 | convolution fusion | flops 5438177280 | bytes 13565952 | tf_op jit(solution)/shard_map/dot_general | solution.py:46
  313.9 10.3 %fusion.55 = bf16[1152,768]{1,0:T(8,128)(2,1)} fusion(bf16[1152,3072]{1,0:T(8,128)(2,1)} %get-tuple-element.261, bf16[1,768,3072]{2,1,0:T(8,128)(2,1)} %param.36), kind=kOutput, calls=%fused_computation.106 | convolution fusion | flops 5436702720 | bytes 13565952 | tf_op jit(solution)/shard_map/dot_general | solution.py:40
  332.3 11.2 %fusion.27 = bf16[1,768,3072]{2,1,0:T(8,128)(2,1)} fusion(bf16[1152,768]{1,0:T(8,128)(2,1)} %bitcast.20, bf16[1152,3072]{1,0:T(8,128)(2,1)} %get-tuple-element.261), kind=kOutput, calls=%fused_computation.70 | convolution fusion | flops 5438177280 | bytes 13565952 | tf_op jit(solution)/shard_map/dot_general | solution.py:46
  372.1 131.4 %while.23 = (s32[]{:T(128)}, bf16[2,576,2304]{2,1,0:T(8,128)(2,1)}, bf16[2,576,768]{1,2,0:T(8,128)(2,1)}, bf16[2,576,768]{1,2,0:T(8,128)(2,1)}, f32[2,12,576]{2,...) while((s32[]{:T(128)}, bf16[2,576,2304]{2,1,0:T(8,128)(2,1)}, ...), condition=%wide.region_19.20_spmd, body=%wide.region_17.19_spmd.sunk | while | flops 2605982976 | bytes 160441552 | solution.py:273
  381.2 7.5 %fusion.155 = f32[12,576,576]{1,2,0:T(8,128)} fusion(bf16[576,12,64]{0,2,1:T(8,128)(2,1)S(1)} %bitcast.156, bf16[576,12,64]{0,2,1:T(8,128)(2,1)S(1)} %bitcast.152), kind=kOutput, calls=%fused_computation.155.clone.1 | convolution fusion | flops 509607936 | bytes 17694720 | tf_op jit(solution)/shard_map/while/body/eval_jaxpr/qhd,khd->hqk/dot_general | solution.py:62
  388.7 10.2 %fusion.156 = bf16[12,64,576]{2,1,0:T(8,128)(2,1)} fusion(bf16[576,12,64]{0,2,1:T(8,128)(2,1)S(1)} %bitcast.154, f32[12,576,576]{1,2,0:T(8,128)} %fusion.155, f32[12,576]{1,0:T(8,128)S(1)} %copy-done.11), kind=kOutput, calls=%fused_computation.21.clone.1 | convolution fusion | flops 521994240 | bytes 17722368 | tf_op jit(solution)/shard_map/while/body/eval_jaxpr/hqk,qhd->khd/dot_general | solution.py:89
  398.9 11.7 %multiply_reduce_fusion.11 = (f32[12,576]{1,0:T(8,128)S(1)}, f32[12,576,576]{1,2,0:T(8,128)}) fusion(f32[12,576,576]{1,2,0:T(8,128)} %fusion.155, f32[12,576]{1,0:T(8,128)S(1)} %copy-done.11, bf16[576,12,64]{0,2,1:T(8,128)(2,1)S(1)} %bitcast.155, bf16[576,12,64]{0,2,1:T(8,128)(2,1)S(1)} %bitcast.160), kind=kOutput, calls=%fused_computation.12.clone.1 | convolution fusion | flops 525526272 | bytes 33675264 | tf_op jit(solution)/shard_map/while/body/eval_jaxpr/qhd,khd->hqk/dot_general | solution.py:86
  410.6 13.3 %multiply_convert_fusion.7 = bf16[12,576,576]{1,2,0:T(8,128)(2,1)S(1)} fusion(f32[12,576,576]{1,2,0:T(8,128)} %get-tuple-element.358, f32[12,576,576]{1,2,0:T(8,128)} %fusion.155, f32[12,576]{1,0:T(8,128)S(1)} %get-tuple-element.359, f32[12,576]{1,0:T(8,128)S(1)} %copy-done.11), kind=kLoop, calls=%fused_computation.11.clone.1 | loop fusion | flops 19906560 | bytes 39868416 | tf_op jit(solution)/shard_map/while/body/eval_jaxpr/convert_element_type | solution.py:94
  447.1 7.5 %fusion.155 = f32[12,576,576]{1,2,0:T(8,128)} fusion(bf16[576,12,64]{0,2,1:T(8,128)(2,1)S(1)} %bitcast.156, bf16[576,12,64]{0,2,1:T(8,128)(2,1)S(1)} %bitcast.152), kind=kOutput, calls=%fused_computation.155.clone.1 | convolution fusion | flops 509607936 | bytes 17694720 | tf_op jit(solution)/shard_map/while/body/eval_jaxpr/qhd,khd->hqk/dot_general | solution.py:62
  454.6 10.2 %fusion.156 = bf16[12,64,576]{2,1,0:T(8,128)(2,1)} fusion(bf16[576,12,64]{0,2,1:T(8,128)(2,1)S(1)} %bitcast.154, f32[12,576,576]{1,2,0:T(8,128)} %fusion.155, f32[12,576]{1,0:T(8,128)S(1)} %copy-done.11), kind=kOutput, calls=%fused_computation.21.clone.1 | convolution fusion | flops 521994240 | bytes 17722368 | tf_op jit(solution)/shard_map/while/body/eval_jaxpr/hqk,qhd->khd/dot_general | solution.py:89
  464.8 11.7 %multiply_reduce_fusion.11 = (f32[12,576]{1,0:T(8,128)S(1)}, f32[12,576,576]{1,2,0:T(8,128)}) fusion(f32[12,576,576]{1,2,0:T(8,128)} %fusion.155, f32[12,576]{1,0:T(8,128)S(1)} %copy-done.11, bf16[576,12,64]{0,2,1:T(8,128)(2,1)S(1)} %bitcast.155, bf16[576,12,64]{0,2,1:T(8,128)(2,1)S(1)} %bitcast.160), kind=kOutput, calls=%fused_computation.12.clone.1 | convolution fusion | flops 525526272 | bytes 33675264 | tf_op jit(solution)/shard_map/while/body/eval_jaxpr/qhd,khd->hqk/dot_general | solution.py:86
  476.6 12.5 %multiply_convert_fusion.7 = bf16[12,576,576]{1,2,0:T(8,128)(2,1)S(1)} fusion(f32[12,576,576]{1,2,0:T(8,128)} %get-tuple-element.358, f32[12,576,576]{1,2,0:T(8,128)} %fusion.155, f32[12,576]{1,0:T(8,128)S(1)} %get-tuple-element.359, f32[12,576]{1,0:T(8,128)S(1)} %copy-done.11), kind=kLoop, calls=%fused_computation.11.clone.1 | loop fusion | flops 19906560 | bytes 39868416 | tf_op jit(solution)/shard_map/while/body/eval_jaxpr/convert_element_type | solution.py:94
  503.5 11.1 %fusion.78 = f32[768,2304]{1,0:T(8,128)} fusion(bf16[1152,2304]{1,0:T(8,128)(2,1)} %bitcast.172, bf16[1152,768]{0,1:T(8,128)(2,1)} %copy.98, f32[768]{0:T(1024)} %param.32, f32[768]{0:T(1024)} %param.31, f32[1152]{0:T(1024)S(1)} %copy-done.39, f32[1152]{0:T(1024)S(1)} %copy-done.32), kind=kOutput, calls=%fused_computation.149 | convolution fusion | flops 4082171904 | bytes 14171136 | tf_op jit(solution)/shard_map/dot_general | solution.py:46
  514.6 9.2 %fusion.85 = (f32[768]{0:T(1024)}, f32[1152,768]{1,0:T(8,128)}) fusion(bf16[1152,2304]{1,0:T(8,128)(2,1)} %bitcast.173, bf16[768,2304]{1,0:T(8,128)(2,1)S(1)} %copy-done), kind=kOutput, calls=%fused_computation.153 | convolution fusion | flops 4077747456 | bytes 12389376 | tf_op jit(solution)/shard_map/dot_general | solution.py:40
  551.8 41.6 %all-reduce = (f32[768]{0:T(1024)}, f32[768]{0:T(1024)}, f32[768]{0:T(1024)}, f32[768]{0:T(1024)}, f32[768]{0:T(1024)}, /*index=5*/f32[768]{0:T(1024)}, f32[768]{0:T(1024)}, f32[768,8]{0,1:T(8,128)}) all-reduce(f32[768]{0:T(1024)S(1)} %get-tuple-element.182, ...), channel_id=1, replica_groups=mesh['rep'=4,'exp'=8] {'rep','exp'}, use_global_device_ids=true, to_apply=%region_24.25 | all-reduce | flops 11520 | bytes 92160 | tf_op jit(solution)/shard_map/psum | solution.py:304
  599.2 106.4 %all-reduce.4.cloned.1.call-done = (f32[768,2304]{1,0:T(8,128)}, f32[768,768]{1,0:T(8,128)}) async-done(((f32[768,2304]{1,0:T(8,128)}, f32[768,768]{1,0:T(8,128)}), (f32[768,2304]{1,0:T(8,128)}, f32[768,768]{1,0:T(8,128)})) %all-reduce.4.cloned.1.call-update) | async-done | bytes 9437200 | tf_op jit(solution)/shard_map/psum | solution.py:304
  705.6 6.6 copy.181
  (255 shorter events, 213.5 us)
Async XLA Ops:
  8.0 12.2 %copy-start = (bf16[768,2304]{1,0:T(8,128)(2,1)S(1)}, bf16[768,2304]{1,0:T(8,128)(2,1)}, u32[]{:S(2)}) copy-start(bf16[768,2304]{1,0:T(8,128)(2,1)} %param.26) | copy-start | bytes 10616836
  12.4 7.8 %copy-start.47 = (f32[768]{0:T(1024)S(1)}, f32[768]{0:T(1024)}, u32[]{:S(2)}) copy-start(f32[768]{0:T(1024)} %param.31) | copy-start | bytes 9220
  12.4 7.9 %copy-start.58 = (f32[768]{0:T(1024)S(1)}, f32[768]{0:T(1024)}, u32[]{:S(2)}) copy-start(f32[768]{0:T(1024)} %param.32) | copy-start | bytes 9220
  18.2 7.7 %copy-start.31 = (f32[1152]{0:T(1024)}, f32[1152]{0:T(1024)S(1)}, u32[]{:S(2)}) copy-start(f32[1152]{0:T(1024)S(1)} %broadcast_multiply_fusion.5) | copy-start | bytes 13828
  40.2 76.2 %copy-start.52 = (f32[768]{0:T(1024)S(1)}, f32[768]{0:T(1024)}, u32[]{:S(2)}) copy-start(f32[768]{0:T(1024)} %convert_element_type.153) | copy-start | bytes 9220
  62.1 11.1 %copy-start.14 = (f32[12,576]{1,0:T(8,128)S(1)}, f32[12,576]{1,0:T(8,128)}, u32[]{:S(2)}) copy-start(f32[12,576]{1,0:T(8,128)} %get-tuple-element.348) | copy-start | bytes 82948 | tf_op jit(solution)/shard_map/while
  62.1 11.1 %copy-start.15 = (f32[12,576]{1,0:T(8,128)S(1)}, f32[12,576]{1,0:T(8,128)}, u32[]{:S(2)}) copy-start(f32[12,576]{1,0:T(8,128)} %fusion.143) | copy-start | bytes 82948 | tf_op jit(solution)/shard_map/while
  62.1 11.1 %copy-start.23 = (f32[2,12,576]{2,1,0:T(8,128)S(1)}, f32[2,12,576]{2,1,0:T(8,128)}, u32[]{:S(2)}) copy-start(f32[2,12,576]{2,1,0:T(8,128)} %get-tuple-element.369) | copy-start | bytes 165892 | tf_op jit(solution)/shard_map/while
  99.8 11.1 %copy-start.14 = (f32[12,576]{1,0:T(8,128)S(1)}, f32[12,576]{1,0:T(8,128)}, u32[]{:S(2)}) copy-start(f32[12,576]{1,0:T(8,128)} %get-tuple-element.348) | copy-start | bytes 82948 | tf_op jit(solution)/shard_map/while
  99.8 11.1 %copy-start.15 = (f32[12,576]{1,0:T(8,128)S(1)}, f32[12,576]{1,0:T(8,128)}, u32[]{:S(2)}) copy-start(f32[12,576]{1,0:T(8,128)} %fusion.143) | copy-start | bytes 82948 | tf_op jit(solution)/shard_map/while
  99.8 11.1 %copy-start.23 = (f32[2,12,576]{2,1,0:T(8,128)S(1)}, f32[2,12,576]{2,1,0:T(8,128)}, u32[]{:S(2)}) copy-start(f32[2,12,576]{2,1,0:T(8,128)} %get-tuple-element.369) | copy-start | bytes 165892 | tf_op jit(solution)/shard_map/while
  126.9 10.1 %copy-start.54 = (bf16[1,768]{1,0:T(2,128)(2,1)S(1)}, bf16[1,768]{1,0:T(2,128)(2,1)}, u32[]{:S(2)}) copy-start(bf16[1,768]{1,0:T(2,128)(2,1)} %param.39) | copy-start | bytes 4612
  127.0 28.7 %all-to-all-start = ((bf16[8,144,768]{2,1,0:T(8,128)(2,1)}), bf16[8,144,768]{2,1,0:T(8,128)(2,1)}, u32[]{:S(2)}, u32[]{:S(2)}) async-start(bf16[8,144,768]{2,1,0:T(8,128)(2,1)} %bitcast.175), calls=%async_computation | async-start | bytes 3538944 | tf_op jit(solution)/shard_map/all_to_all | solution.py:187
  133.1 22.6 %copy-start.50 = (f32[1,3072]{1,0:T(1,128)S(1)}, f32[1,3072]{1,0:T(1,128)}, u32[]{:S(2)}) copy-start(f32[1,3072]{1,0:T(1,128)} %add.177) | copy-start | bytes 36868
  155.7 40.7 %copy-start.51 = (f32[768]{0:T(1024)S(1)}, f32[768]{0:T(1024)}, u32[]{:S(2)}) copy-start(f32[768]{0:T(1024)} %convert_reduce_fusion.2) | copy-start | bytes 9220
  155.7 40.7 %copy-start.55 = (bf16[1,3072,768]{2,1,0:T(8,128)(2,1)S(1)}, bf16[1,3072,768]{2,1,0:T(8,128)(2,1)}, u32[]{:S(2)}) copy-start(bf16[1,3072,768]{2,1,0:T(8,128)(2,1)} %param.38) | copy-start | bytes 14155780
  203.2 27.6 %all-to-all-start.1 = ((bf16[8,144,768]{2,1,0:T(8,128)(2,1)}), bf16[8,144,768]{2,1,0:T(8,128)(2,1)}, u32[]{:S(2)}, u32[]{:S(2)}) async-start(bf16[8,144,768]{2,1,0:T(8,128)(2,1)} %bitcast.176), calls=%async_computation.1 | async-start | bytes 3538944 | tf_op jit(solution)/shard_map/all_to_all | solution.py:199
  207.7 135.9 %reduce-scatter.15.cloned.1.call-start = ((), (), s32[]{:S(2)}) async-start(), calls=%async_computation.11 | async-start | bytes 245760
  230.8 8.0 %copy-start.9 = (bf16[1152,768]{0,1:T(8,128)(2,1)S(1)}, bf16[1152,768]{0,1:T(8,128)(2,1)}, u32[]{:S(2)}) copy-start(bf16[1152,768]{0,1:T(8,128)(2,1)} %copy.103) | copy-start | bytes 5308420
  278.8 67.6 %reduce-scatter.13.cloned.1.call-start = ((), (), s32[]{:S(2)}) async-start(), calls=%async_computation.10 | async-start | bytes 983040
  301.7 291.7 %reduce-scatter.11.cloned.1.call-start = ((), (), s32[]{:S(2)}) async-start(), calls=%async_computation.9 | async-start | bytes 5898240 | tf_op jit(solution)/shard_map/reduce_scatter | solution.py:249
  324.2 27.6 %all-to-all-start.3 = ((bf16[8,144,768]{2,1,0:T(8,128)(2,1)}), bf16[8,144,768]{2,1,0:T(8,128)(2,1)}, u32[]{:S(2)}, u32[]{:S(2)}) async-start(bf16[8,144,768]{2,1,0:T(8,128)(2,1)} %bitcast.174), calls=%async_computation.3 | async-start | bytes 3538944 | tf_op jit(solution)/shard_map/all_to_all | solution.py:235
  328.7 267.6 %reduce-scatter.9.cloned.1.call-start = ((), (), s32[]{:S(2)}) async-start(), calls=%async_computation.8 | async-start | bytes 5898240 | tf_op jit(solution)/shard_map/reduce_scatter | solution.py:243
  343.5 362.0 %all-reduce.4.cloned.1.call-start = ((), (), s32[]{:S(2)}) async-start(), calls=%async_computation.12 | async-start | bytes 18874368 | tf_op jit(solution)/shard_map/psum | solution.py:304
  351.8 10.1 %slice-start = ((s8[7077888]{0:T(1024)(128)(4,1)}), s8[4194304]{0:T(1024)(128)(4,1)S(1)}, s32[]{:S(2)}) async-start(s8[7077888]{0:T(1024)(128)(4,1)} %bitcast.164), calls=%async_computation.13 | async-start | bytes 8388608
  351.9 10.0 %slice-start.1 = ((s8[7077888]{0:T(1024)(128)(4,1)}), s8[2883584]{0:T(1024)(128)(4,1)S(1)}, s32[]{:S(2)}) async-start(s8[7077888]{0:T(1024)(128)(4,1)} %bitcast.164), calls=%async_computation.14 | async-start | bytes 5767168
  372.1 131.4 %copy-start.32 = (f32[1152]{0:T(1024)S(1)}, f32[1152]{0:T(1024)}, u32[]{:S(2)}) copy-start(f32[1152]{0:T(1024)} %copy-done.31) | copy-start | bytes 13828
  372.1 131.4 %copy-start.39 = (f32[1152]{0:T(1024)S(1)}, f32[1152]{0:T(1024)}, u32[]{:S(2)}) copy-start(f32[1152]{0:T(1024)} %copy-done.38) | copy-start | bytes 13828
  381.2 7.5 %copy-start.1 = (bf16[1,576,768]{1,2,0:T(8,128)(2,1)S(1)}, bf16[1,576,768]{1,2,0:T(8,128)(2,1)}, u32[]{:S(2)}) copy-start(bf16[1,576,768]{1,2,0:T(8,128)(2,1)} %copy.157) | copy-start | bytes 2654212 | tf_op jit(solution)/shard_map/while
  381.2 7.5 %copy-start.11 = (f32[12,576]{1,0:T(8,128)S(1)}, f32[12,576]{1,0:T(8,128)}, u32[]{:S(2)}) copy-start(f32[12,576]{1,0:T(8,128)} %dynamic-slice_bitcast_fusion.2) | copy-start | bytes 82948 | tf_op jit(solution)/shard_map/while
  447.0 7.6 %copy-start.1 = (bf16[1,576,768]{1,2,0:T(8,128)(2,1)S(1)}, bf16[1,576,768]{1,2,0:T(8,128)(2,1)}, u32[]{:S(2)}) copy-start(bf16[1,576,768]{1,2,0:T(8,128)(2,1)} %copy.157) | copy-start | bytes 2654212 | tf_op jit(solution)/shard_map/while
  447.1 7.6 %copy-start.11 = (f32[12,576]{1,0:T(8,128)S(1)}, f32[12,576]{1,0:T(8,128)}, u32[]{:S(2)}) copy-start(f32[12,576]{1,0:T(8,128)} %dynamic-slice_bitcast_fusion.2) | copy-start | bytes 82948 | tf_op jit(solution)/shard_map/while
  (45 other events, 157.1 us)
Sparse Core Ops, SparseCore 0:
  278.9 19.2 reduce-scatter.14
  301.9 23.1 reduce-scatter.12
  327.4 84.5 reduce-scatter.10
  414.1 85.8 reduce-scatter.8
Sparse Core Ops, SparseCore 1:
  514.7 190.8 all-reduce.3
where the time goes:
time: 728 us; the launch traced here: 721 us
  matrix products  275 us (38%)
  waiting for transfers between devices  141 us (19%)
  local copies, waits for them, and re-layouts  108 us (15%)
  other arithmetic  96.2 us (13%)
  blocking collectives  67.9 us (9%)
  between operations  16.1 us (2%)
  starting transfers between devices  14.7 us (2%)
    psum x1, waiting for transfers between devices, on_device(): lax.psum((local_qkv, local_q_bias, local_v_bias, local_proj, local_proj_b...  106 us
    unnamed x123, local copies, waits for them, and re-layouts  48.4 us
    dot_general x6, matrix products, contract_first(): lax.dot_general(left, right, (((0,), (0,)), ((), ())), preferred_element_...  44.9 us
    dot_general x4, matrix products, contract_last(): lax.dot_general(left, right, (((1,), (1,)), ((), ())), preferred_element_...  43.2 us
    psum x1, blocking collectives, on_device(): lax.psum((local_qkv, local_q_bias, local_v_bias, local_proj, local_proj_b...  41.6 us
    dot_general x1, matrix products, on_device(): jnp.dot(arrived, weight_in, preferred_element_type=jnp.float32) + bias_in  40.7 us
    dot_general x4, matrix products, image_scores(): jnp.einsum('qhd,khd->hqk', by_heads(queries), by_heads(key_rows), preferr...  31.1 us
    all_to_all x1, blocking collectives, on_device(): lax.all_to_all(grad_returned, 'exp', split_axis=0, concat_axis=0, tiled=T...  26.2 us
  transfers between devices with their start and end apart: 8, of which 4 were waited for; matrix products, arithmetic and copies ran while one was open for 39% of the time, Pallas kernels for 0%

commit v1 on v0

v1 whole, which is shorter than its diff:
```python
import functools

import jax
import jax.numpy as jnp
from jax import lax
from jax.experimental import pallas as pl
from jax.experimental.pallas import tpu as pltpu
from jax.sharding import PartitionSpec as P

HEAD_DIM = 64
SEQ = 576
PAIR = 2 * HEAD_DIM
SPLIT = 512
AUX = 128
EPSILON = 1e-06
F32 = jnp.float32
BF16 = jnp.bfloat16
VMEM_BYTES = 56 * 2**20


def dot(left, right):
    return lax.dot_general(left, right, (((1,), (0,)), ((), ())), preferred_element_type=F32)


def dot_last(left, right):
    return lax.dot_general(left, right, (((1,), (1,)), ((), ())), preferred_element_type=F32)


def dot_first(left, right):
    return lax.dot_general(left, right, (((0,), (0,)), ((), ())), preferred_element_type=F32)


def thirds(value):
    high = value.astype(BF16)
    rest = value - high.astype(F32)
    middle = rest.astype(BF16)
    return high, middle, (rest - middle.astype(F32)).astype(BF16)


def standardize(field):
    centred = field - jnp.mean(field, axis=-1, keepdims=True)
    inverse = lax.rsqrt(jnp.mean(centred * centred, axis=-1, keepdims=True) + EPSILON)
    return centred * inverse, inverse


def standardize_back(grad, gain, unit, inverse):
    scaled = grad * gain
    along = jnp.mean(scaled * unit, axis=-1, keepdims=True)
    return inverse * (scaled - jnp.mean(scaled, axis=-1, keepdims=True) - unit * along)


def column_sum(field):
    return jnp.sum(field, axis=0, keepdims=True)


def params():
    return pltpu.CompilerParams(vmem_limit_bytes=VMEM_BYTES)


def whole(array):
    return pl.BlockSpec(array.shape, lambda *ids: (0,) * array.ndim)


def shape(dims, kind):
    return jax.ShapeDtypeStruct(dims, kind)


def split_heads(pair):
    lane = lax.broadcasted_iota(jnp.int32, pair.shape, 1)
    zero = jnp.zeros_like(pair)
    first = jnp.where(lane < HEAD_DIM, pair, zero)
    second = jnp.where(lane < HEAD_DIM, zero, pair)
    return jnp.concatenate([first[:SPLIT], second[:SPLIT], first[SPLIT:], second[SPLIT:]], axis=0)


def key_sides():
    row = lax.broadcasted_iota(jnp.int32, (2 * SEQ, PAIR), 0)
    lane = lax.broadcasted_iota(jnp.int32, (2 * SEQ, PAIR), 1)
    is_first = (row < SPLIT) | ((row >= 2 * SPLIT) & (row < SPLIT + SEQ))
    return is_first, lane


def front_kernel(
    chunk,
    tokens,
    w_qkv,
    bias,
    w_proj,
    proj_bias,
    gain_one,
    shift_one,
    gain_two,
    shift_two,
    w_router,
    normed_one_out,
    qkv_out,
    weights_out,
    inverse_out,
    context_out,
    residual_out,
    normed_two_out,
    router_out,
    value_side,
):
    pair = pl.program_id(1)
    pairs = context_out.shape[1]

    @pl.when((pl.program_id(0) == 0) & (pair == 0))
    def _():
        is_first, lane = key_sides()
        value_side[:, PAIR:] = jnp.where(is_first == (lane < HEAD_DIM), 1.0, 0.0).astype(BF16)

    @pl.when(pair == 0)
    def _():
        unit, _ = standardize(tokens[...].astype(F32))
        normed = (unit * gain_one[...] + shift_one[...]).astype(BF16)
        normed_one_out[...] = normed
        width = w_qkv.shape[1]
        step = 2 * PAIR
        for at in range(0, width, step):
            part = dot(normed, w_qkv[:, at : at + step]) + bias[:, at : at + step]
            part = part.astype(BF16)
            if at < width // 3:
                part = part * jnp.asarray(HEAD_DIM**-0.5, BF16)
            qkv_out[0, at // PAIR] = part[:, :PAIR]
            qkv_out[0, at // PAIR + 1] = part[:, PAIR:]

    keys = split_heads(qkv_out[0, pairs + pair])
    value_side[:, :PAIR] = split_heads(qkv_out[0, 2 * pairs + pair])
    values = value_side[...]
    low = lax.broadcasted_iota(jnp.int32, (chunk, PAIR), 1) < HEAD_DIM
    for at in range(0, SEQ, chunk):
        rows = slice(at, at + chunk)
        scores = dot_last(qkv_out[0, pair, rows], keys)
        first = scores[:, :SPLIT]
        second = scores[:, SPLIT : 2 * SPLIT]
        tail = scores[:, 2 * SPLIT :]
        first_max = jnp.maximum(
            jnp.max(first, axis=1, keepdims=True),
            jnp.max(jnp.where(low, tail, -jnp.inf), axis=1, keepdims=True),
        )
        second_max = jnp.maximum(
            jnp.max(second, axis=1, keepdims=True),
            jnp.max(jnp.where(low, -jnp.inf, tail), axis=1, keepdims=True),
        )
        exponent = jnp.concatenate(
            [
                jnp.exp(first - first_max).astype(BF16),
                jnp.exp(second - second_max).astype(BF16),
                jnp.exp(tail - jnp.where(low, first_max, second_max)).astype(BF16),
            ],
            axis=1,
        )
        weights_out[0, 0, rows] = exponent
        summed = dot(exponent, values)
        inverse = 1.0 / summed[:, PAIR:]
        inverse_out[0, 0, rows] = inverse
        context_out[0, pair, rows] = (summed[:, :PAIR] * inverse).astype(BF16)

    @pl.when(pair == pairs - 1)
    def _():
        context = jnp.concatenate([context_out[0, at] for at in range(pairs)], axis=1)
        residual = tokens[...].astype(F32) + (dot(context, w_proj[...]) + proj_bias[...])
        residual_out[...] = residual
        unit, _ = standardize(residual)
        normed = (unit * gain_two[...] + shift_two[...]).astype(BF16)
        normed_two_out[...] = normed
        high, middle, rest = thirds(w_router[...])
        logits = dot(normed, high) + (dot(normed, middle) + dot(normed, rest))
        exponent = jnp.exp(logits - jnp.max(logits, axis=1, keepdims=True))
        router_out[...] = exponent / jnp.sum(exponent, axis=1, keepdims=True)


def front(tokens, w_qkv, bias, w_proj, proj_bias, gain_one, shift_one, gain_two, shift_two, w_router):
    rows, width = tokens.shape
    images = rows // SEQ
    pairs = width // PAIR
    experts = w_router.shape[1]

    def per_image(columns):
        return pl.BlockSpec((SEQ, columns), lambda i, p: (i, 0))

    fixed = (w_qkv, bias, w_proj, proj_bias, gain_one, shift_one, gain_two, shift_two, w_router)
    return pl.pallas_call(
        functools.partial(front_kernel, SEQ // 2),
        grid=(images, pairs),
        in_specs=[per_image(width)] + [whole(array) for array in fixed],
        out_specs=[
            per_image(width),
            pl.BlockSpec((1, 3 * pairs, SEQ, PAIR), lambda i, p: (i, 0, 0, 0)),
            pl.BlockSpec((1, 1, SEQ, 2 * SEQ), lambda i, p: (i, p, 0, 0)),
            pl.BlockSpec((1, 1, SEQ, PAIR), lambda i, p: (i, p, 0, 0)),
            pl.BlockSpec((1, pairs, SEQ, PAIR), lambda i, p: (i, 0, 0, 0)),
            per_image(width),
            per_image(width),
            per_image(experts),
        ],
        out_shape=[
            shape((rows, width), BF16),
            shape((images, 3 * pairs, SEQ, PAIR), BF16),
            shape((images, pairs, SEQ, 2 * SEQ), BF16),
            shape((images, pairs, SEQ, PAIR), F32),
            shape((images, pairs, SEQ, PAIR), BF16),
            shape((rows, width), F32),
            shape((rows, width), BF16),
            shape((rows, experts), F32),
        ],
        scratch_shapes=[pltpu.VMEM((2 * SEQ, 2 * PAIR), BF16)],
        compiler_params=params(),
        name="front",
    )(tokens, *fixed)


def slot_hits(columns, chunk):
    at = pl.program_id(0) * chunk
    slot = at + lax.broadcasted_iota(jnp.int32, (chunk, columns.shape[1]), 0)
    hit = (columns[0:1, :] == slot) | (columns[1:2, :] == slot)
    return jnp.where(hit, 1.0, 0.0).astype(BF16)


def gather_kernel(chunk, columns, rows, out):
    out[...] = dot(slot_hits(columns, chunk), rows[...]).astype(BF16)


def gather(columns, rows, chunk=288):
    count, width = rows.shape
    return pl.pallas_call(
        functools.partial(gather_kernel, chunk),
        grid=(count // chunk,),
        in_specs=[whole(columns), whole(rows)],
        out_specs=pl.BlockSpec((chunk, width), lambda i: (i, 0)),
        out_shape=shape((count, width), BF16),
        compiler_params=params(),
        name="gather",
    )(columns, rows)


def dispatch_kernel(chunk, slot_count, columns, rows, router, out):
    hits = slot_hits(columns, chunk)
    width = rows.shape[1]
    experts = router.shape[1]
    out[:, :width] = dot(hits, rows[...]).astype(BF16)
    high, middle, rest = thirds(router[...])
    gates = dot(hits, high) + (dot(hits, middle) + dot(hits, rest))
    slot = pl.program_id(0) * chunk + lax.broadcasted_iota(jnp.int32, (chunk, experts), 0)
    start = lax.broadcasted_iota(jnp.int32, (chunk, experts), 1) * slot_count
    own = (slot >= start) & (slot < start + slot_count)
    gate = jnp.sum(jnp.where(own, gates, 0.0), axis=1, keepdims=True)
    out[:, width:] = spread(gate)


def spread(column):
    high, middle, rest = thirds(jnp.broadcast_to(column, (column.shape[0], AUX)))
    lane = lax.broadcasted_iota(jnp.int32, (column.shape[0], AUX), 1)
    zero = jnp.zeros_like(high)
    return jnp.where(lane == 0, high, jnp.where(lane == 1, middle, jnp.where(lane == 2, rest, zero)))


def unspread(block):
    return jnp.sum(block.astype(F32), axis=1, keepdims=True)


def dispatch(columns, rows, router, slot_count, chunk=288):
    count, width = rows.shape
    return pl.pallas_call(
        functools.partial(dispatch_kernel, chunk, slot_count),
        grid=(count // chunk,),
        in_specs=[whole(columns), whole(rows), whole(router)],
        out_specs=pl.BlockSpec((chunk, width + AUX), lambda i: (i, 0)),
        out_shape=shape((count, width + AUX), BF16),
        compiler_params=params(),
        name="dispatch",
    )(columns, rows, router)


def raw_kernel(cotangent, weight_out, out):
    out[...] = dot_last(cotangent[...], weight_out[...]).astype(BF16)


def raw_active(cotangent, weight_out, chunk=512):
    count, width = cotangent.shape
    hidden = weight_out.shape[0]
    return pl.pallas_call(
        raw_kernel,
        grid=(hidden // chunk,),
        in_specs=[whole(cotangent), pl.BlockSpec((chunk, width), lambda i: (i, 0))],
        out_specs=pl.BlockSpec((count, chunk), lambda i: (0, i)),
        out_shape=shape((count, hidden), BF16),
        compiler_params=params(),
        name="raw_active",
    )(cotangent, weight_out)


def expert_kernel(
    row_chunk,
    arrived,
    cotangent,
    weight_in,
    bias_in,
    raw,
    bias_out,
    active_out,
    hidden_out,
    weight_grad,
    bias_grad,
    out_bias_grad,
    back,
    produced_grad,
    total,
    gate_total,
):
    step = pl.program_id(0)
    count, width = cotangent.shape

    @pl.when(step == 0)
    def _():
        gate = unspread(arrived[:, width:])
        gated = (gate * cotangent[...].astype(F32)).astype(BF16)
        produced_grad[...] = gated
        out_bias_grad[...] = column_sum(gated.astype(F32))
        total[...] = jnp.zeros_like(total)
        gate_total[...] = jnp.broadcast_to(
            jnp.sum(cotangent[...].astype(F32) * bias_out[...], axis=1, keepdims=True), gate_total.shape
        )

    sums = jnp.zeros(bias_grad.shape, F32)
    for at in range(0, count, row_chunk):
        rows = slice(at, at + row_chunk)
        gate = unspread(arrived[rows, width:])
        hidden = dot(arrived[rows, :width], weight_in[...]) + bias_in[...]
        cdf = 0.5 + 0.5 * lax.erf(hidden * (0.5**0.5))
        density = jnp.exp(hidden * hidden * -0.5) * (0.5 * 1.1283791670955126 * 0.5**0.5)
        active = (hidden * cdf).astype(BF16)
        incoming = raw[rows, :].astype(F32)
        gate_total[rows, :] += jnp.sum(active.astype(F32) * incoming, axis=1, keepdims=True)
        grad = (incoming * gate * (cdf + hidden * density)).astype(BF16)
        active_out[rows, :] = active
        hidden_out[rows, :] = grad
        sums += column_sum(grad.astype(F32))
        total[rows, :] += dot_last(grad, weight_in[...])
    bias_grad[...] = sums
    weight_grad[...] = dot_first(active_out[...], produced_grad[...]).astype(BF16)

    @pl.when(step == pl.num_programs(0) - 1)
    def _():
        back[:, :width] = total[...].astype(BF16)
        back[:, width:] = spread(gate_total[:, 0:1])


def expert(arrived, cotangent, weight_in, bias_in, raw, bias_out, chunk=512):
    count, width = cotangent.shape
    hidden = weight_in.shape[1]

    def column_block(rows):
        return pl.BlockSpec((rows, chunk), lambda i: (0, i))

    return pl.pallas_call(
        functools.partial(expert_kernel, 288),
        grid=(hidden // chunk,),
        in_specs=[
            whole(arrived),
            whole(cotangent),
            column_block(width),
            column_block(1),
            column_block(count),
            whole(bias_out),
        ],
        out_specs=[
            column_block(count),
            column_block(count),
            pl.BlockSpec((chunk, width), lambda i: (i, 0)),
            column_block(1),
            pl.BlockSpec((1, width), lambda i: (0, 0)),
            pl.BlockSpec((count, width + AUX), lambda i: (0, 0)),
        ],
        out_shape=[
            shape((count, hidden), BF16),
            shape((count, hidden), BF16),
            shape((hidden, width), BF16),
            shape((1, hidden), F32),
            shape((1, width), F32),
            shape((count, width + AUX), BF16),
        ],
        scratch_shapes=[
            pltpu.VMEM((count, width), BF16),
            pltpu.VMEM((count, width), F32),
            pltpu.VMEM((count, 128), F32),
        ],
        compiler_params=params(),
        name="expert",
    )(arrived, cotangent, weight_in, bias_in, raw, bias_out)


def weight_in_kernel(arrived, grad_hidden, bias_grad, out_bias_grad, out, turned):
    width = turned.shape[0]

    @pl.when(pl.program_id(0) == 0)
    def _():
        turned[...] = arrived[:, :width].T

    out[0, :width] = dot(turned[...], grad_hidden[...]).astype(BF16)
    row = lax.broadcasted_iota(jnp.int32, (out.shape[1] - width, out.shape[2]), 0)
    out[0, width:] = jnp.where(row == 0, bias_grad[...], jnp.where(row == 1, out_bias_grad[0], 0.0)).astype(BF16)


def weight_in_grad(arrived, grad_hidden, bias_grad, out_bias_grad, width, reps):
    count, hidden = grad_hidden.shape
    part = hidden // reps
    return pl.pallas_call(
        weight_in_kernel,
        grid=(reps,),
        in_specs=[
            whole(arrived),
            pl.BlockSpec((count, part), lambda i: (0, i)),
            pl.BlockSpec((1, part), lambda i: (0, i)),
            pl.BlockSpec((1, 1, part), lambda i: (i, 0, 0)),
        ],
        out_specs=pl.BlockSpec((1, width + 16, part), lambda i: (i, 0, 0)),
        out_shape=shape((reps, width + 16, part), BF16),
        scratch_shapes=[pltpu.VMEM((width, count), BF16)],
        compiler_params=params(),
        name="weight_in_grad",
    )(arrived, grad_hidden, bias_grad, out_bias_grad)


def produce_kernel(arrived, active, weight_out, bias_out, out):
    gate = unspread(arrived[...])
    out[...] = (gate * (dot(active[...], weight_out[...]) + bias_out[...])).astype(BF16)


def produce(arrived, active, weight_out, bias_out, chunk=288):
    count, hidden = active.shape
    width = weight_out.shape[1]
    return pl.pallas_call(
        produce_kernel,
        grid=(count // chunk,),
        in_specs=[
            pl.BlockSpec((chunk, AUX), lambda i: (i, width // AUX)),
            pl.BlockSpec((chunk, hidden), lambda i: (i, 0)),
            whole(weight_out),
            whole(bias_out),
        ],
        out_specs=pl.BlockSpec((chunk, width), lambda i: (i, 0)),
        out_shape=shape((count, width), BF16),
        compiler_params=params(),
        name="produce",
    )(arrived, active, weight_out, bias_out)


def token_hits(columns, slots):
    slot = lax.broadcasted_iota(jnp.int32, (columns.shape[0], slots), 1)
    hit = (columns[:, 0:1] == slot) | (columns[:, 1:2] == slot)
    return jnp.where(hit, 1.0, 0.0).astype(BF16)


def middle_kernel(
    slot_count,
    columns,
    source,
    router,
    normed_two,
    residual,
    cotangent,
    context,
    w_router,
    w_proj,
    gain_two,
    grad_residual_out,
    grad_context_out,
    proj_grad,
    vectors,
    router_grad,
    gate_side,
    proj_total,
):
    image = pl.program_id(0)
    slots = source.shape[0]
    experts, width = w_router.shape
    pairs = context.shape[1]

    @pl.when(image == 0)
    def _():
        gate = unspread(source[:, width:])
        slot = lax.broadcasted_iota(jnp.int32, (slots, experts), 0)
        start = lax.broadcasted_iota(jnp.int32, (slots, experts), 1) * slot_count
        own = (slot >= start) & (slot < start + slot_count)
        for at, part in enumerate(thirds(jnp.where(own, gate, 0.0))):
            gate_side[at] = part
        vectors[...] = jnp.zeros_like(vectors)
        router_grad[...] = jnp.zeros_like(router_grad)
        proj_total[...] = jnp.zeros_like(proj_total)

    hits = token_hits(columns, slots)
    grad_router = dot(hits, gate_side[0]) + (dot(hits, gate_side[1]) + dot(hits, gate_side[2]))
    probs = router[...]
    grad_logits = probs * (grad_router - jnp.sum(probs * grad_router, axis=1, keepdims=True))
    left = thirds(grad_logits)
    right = thirds(w_router[...])
    logits_part = dot(left[0], right[0])
    for one, other in ((0, 1), (1, 0), (1, 1), (0, 2), (2, 0)):
        logits_part += dot(left[one], right[other])
    grad_normed = dot(hits, source[:, :width]) + logits_part
    for part in left:
        router_grad[...] += dot_first(part, normed_two[...])
    unit, inverse = standardize(residual[...])
    grad_residual = cotangent[...].astype(F32) + standardize_back(grad_normed, gain_two[...], unit, inverse)
    grad_residual_out[...] = grad_residual
    branch = grad_residual.astype(BF16)
    vectors[0:1] += column_sum(grad_normed * unit)
    vectors[1:2] += column_sum(grad_normed)
    vectors[2:3] += column_sum(branch.astype(F32))
    for pair in range(pairs):
        rows = slice(pair * PAIR, (pair + 1) * PAIR)
        grad_context_out[0, pair] = dot_last(branch, w_proj[rows, :]).astype(BF16)
        proj_total[rows, :] += dot_first(context[0, pair], branch)
    proj_grad[...] = proj_total[...].astype(BF16)


def middle(columns, source, router, normed_two, residual, cotangent, context, w_router, w_proj, gain_two, slot_count):
    rows, width = residual.shape
    images, pairs = context.shape[:2]
    experts = router.shape[1]

    def per_image(columns):
        return pl.BlockSpec((SEQ, columns), lambda i: (i, 0))

    by_pair = pl.BlockSpec((1, pairs, SEQ, PAIR), lambda i: (i, 0, 0, 0))
    turned = w_router.T
    return pl.pallas_call(
        functools.partial(middle_kernel, slot_count),
        grid=(images,),
        in_specs=[
            per_image(2),
            whole(source),
            per_image(experts),
            per_image(width),
            per_image(width),
            per_image(width),
            by_pair,
            whole(turned),
            whole(w_proj),
            whole(gain_two),
        ],
        out_specs=[
            per_image(width),
            by_pair,
            pl.BlockSpec((width, width), lambda i: (0, 0)),
            pl.BlockSpec((8, width), lambda i: (0, 0)),
            pl.BlockSpec((experts, width), lambda i: (0, 0)),
        ],
        out_shape=[
            shape((rows, width), F32),
            shape((images, pairs, SEQ, PAIR), BF16),
            shape((width, width), BF16),
            shape((8, width), F32),
            shape((experts, width), F32),
        ],
        scratch_shapes=[pltpu.VMEM((3, rows, experts), BF16), pltpu.VMEM((width, width), F32)],
        compiler_params=params(),
        name="middle",
    )(columns, source, router, normed_two, residual, cotangent, context, turned, w_proj, gain_two)


def merge_heads(turned):
    first = jnp.concatenate([turned[:HEAD_DIM, :SPLIT], turned[:HEAD_DIM, 2 * SPLIT : SPLIT + SEQ]], axis=1)
    second = jnp.concatenate([turned[HEAD_DIM:, SPLIT : 2 * SPLIT], turned[HEAD_DIM:, SPLIT + SEQ :]], axis=1)
    return jnp.concatenate([first, second], axis=0).T


def attend_back_kernel(
    chunk,
    grad_context,
    queries,
    keys,
    values,
    weights,
    inverse,
    context,
    normed_one,
    grad_out,
    weight_grad,
    value_side,
    grad_scores,
):
    pair = pl.program_id(0)
    image = pl.program_id(1)

    @pl.when((pair == 0) & (image == 0))
    def _():
        is_first, lane = key_sides()
        taken = (is_first & (lane < 2)) | (jnp.logical_not(is_first) & (lane >= 2) & (lane < 4))
        value_side[:, PAIR:] = jnp.where(taken, -1.0, 0.0).astype(BF16)

    key_side = split_heads(keys[0, 0])
    value_side[:, :PAIR] = split_heads(values[0, 0])
    lane = lax.broadcasted_iota(jnp.int32, (chunk, PAIR), 1)
    low = lane < HEAD_DIM
    scaled = []
    for at in range(0, SEQ, chunk):
        rows = slice(at, at + chunk)
        grads = (grad_context[0, 0, rows].astype(F32) * inverse[0, 0, rows]).astype(BF16)
        scaled.append(grads)
        product = grads.astype(F32) * context[0, 0, rows].astype(F32)
        first = jnp.sum(jnp.where(low, product, 0.0), axis=1, keepdims=True)
        second = jnp.sum(jnp.where(low, 0.0, product), axis=1, keepdims=True)
        offset = jnp.where(lane < 2, first, second)
        high = offset.astype(BF16).astype(F32)
        extra = jnp.where(
            (lane == 0) | (lane == 2), high, jnp.where((lane == 1) | (lane == 3), offset - high, 0.0)
        ).astype(BF16)
        grad_weights = dot_last(jnp.concatenate([grads, extra], axis=1), value_side[...])
        part = grad_weights.astype(BF16) * weights[0, 0, rows]
        grad_scores[rows] = part
        place = pl.ds(pl.multiple_of(image * SEQ + at, 32), chunk)
        grad_out[0, pair, place] = (dot(part, key_side) * HEAD_DIM**-0.5).astype(BF16)
    grads = jnp.concatenate(scaled, axis=0)
    place = pl.ds(pl.multiple_of(image * SEQ, 64), SEQ)
    grad_out[1, pair, place] = merge_heads(dot_first(queries[0, 0], grad_scores[...])).astype(BF16)
    grad_out[2, pair, place] = merge_heads(dot_first(grads, weights[0, 0])).astype(BF16)

    @pl.when((pair == pl.num_programs(0) - 1) & (image == pl.num_programs(1) - 1))
    def _():
        for kind in range(3):
            joined = jnp.concatenate([grad_out[kind, at] for at in range(grad_out.shape[1])], axis=1)
            weight_grad[kind] = dot_first(normed_one[...], joined).astype(BF16)


def attend_back(grad_context, qkv, weights, inverse, context, normed_one, first, count):
    images, pairs = context.shape[:2]
    rows, width = normed_one.shape

    def block(offset):
        return pl.BlockSpec((1, 1, SEQ, PAIR), lambda p, i: (i, offset + p, 0, 0))

    return pl.pallas_call(
        functools.partial(attend_back_kernel, SEQ),
        grid=(count, images),
        in_specs=[
            block(first),
            block(first),
            block(pairs + first),
            block(2 * pairs + first),
            pl.BlockSpec((1, 1, SEQ, 2 * SEQ), lambda p, i: (i, first + p, 0, 0)),
            block(first),
            block(first),
            whole(normed_one),
        ],
        out_specs=[
            pl.BlockSpec((3, count, rows, PAIR), lambda p, i: (0, 0, 0, 0)),
            pl.BlockSpec((3, width, count * PAIR), lambda p, i: (0, 0, 0)),
        ],
        out_shape=[shape((3, count, rows, PAIR), BF16), shape((3, width, count * PAIR), BF16)],
        scratch_shapes=[pltpu.VMEM((2 * SEQ, 2 * PAIR), BF16), pltpu.VMEM((SEQ, 2 * SEQ), BF16)],
        compiler_params=params(),
        name="attend_back",
    )(grad_context, qkv, qkv, qkv, weights, inverse, context, normed_one)


def last_kernel(tokens, grad_qkv, w_qkv, grad_residual, gain_one, out, vectors):
    width = tokens.shape[1]
    pairs = width // PAIR

    @pl.when(pl.program_id(0) == 0)
    def _():
        vectors[...] = jnp.zeros_like(vectors)

    unit, inverse = standardize(tokens[...].astype(F32))
    grad_normed = jnp.zeros(tokens.shape, F32)
    for kind in range(3):
        joined = jnp.concatenate([grad_qkv[kind, at] for at in range(pairs)], axis=1)
        grad_normed += dot_last(joined, w_qkv[:, kind * width : (kind + 1) * width])
        if kind == 0:
            vectors[2:3] += column_sum(joined.astype(F32))
        if kind == 2:
            vectors[3:4] += column_sum(joined.astype(F32))
    out[...] = grad_residual[...] + standardize_back(grad_normed, gain_one[...], unit, inverse)
    vectors[0:1] += column_sum(grad_normed * unit)
    vectors[1:2] += column_sum(grad_normed)


def last(tokens, grad_qkv, w_qkv, grad_residual, gain_one):
    rows, width = tokens.shape
    pairs = width // PAIR
    per_image = pl.BlockSpec((SEQ, width), lambda i: (i, 0))
    return pl.pallas_call(
        last_kernel,
        grid=(rows // SEQ,),
        in_specs=[
            per_image,
            pl.BlockSpec((3, pairs, SEQ, PAIR), lambda i: (0, 0, i, 0)),
            whole(w_qkv),
            per_image,
            whole(gain_one),
        ],
        out_specs=[per_image, pl.BlockSpec((8, width), lambda i: (0, 0))],
        out_shape=[shape((rows, width), F32), shape((8, width), F32)],
        compiler_params=params(),
        name="last",
    )(tokens, grad_qkv, w_qkv, grad_residual, gain_one)


def combine_kernel(columns, source, residual, out):
    hits = token_hits(columns, source.shape[0])
    out[...] = (residual[...] + dot(hits, source[...])).astype(BF16)


def combine(columns, source, residual, chunk=288):
    rows, width = residual.shape
    return pl.pallas_call(
        combine_kernel,
        grid=(rows // chunk,),
        in_specs=[
            pl.BlockSpec((chunk, 2), lambda i: (i, 0)),
            whole(source),
            pl.BlockSpec((chunk, width), lambda i: (i, 0)),
        ],
        out_specs=pl.BlockSpec((chunk, width), lambda i: (i, 0)),
        out_shape=shape((rows, width), BF16),
        compiler_params=params(),
        name="combine",
    )(columns, source, residual)


def exchange(rows, experts):
    blocks = rows.reshape(experts, rows.shape[0] // experts, rows.shape[1])
    return lax.all_to_all(blocks, "exp", split_axis=0, concat_axis=0, tiled=True).reshape(rows.shape)


def axis_steps(sizes, swap):
    steps = []
    for name in ("exp", "rep"):
        bits = []
        bit = 1
        while bit < sizes[name]:
            bits.append((name, bit))
            bit *= 2
        if swap and name == "exp" and len(bits) > 2:
            bits[1], bits[2] = bits[2], bits[1]
        steps += bits
    return steps


def sum_everywhere(block, sizes, swap):
    steps = axis_steps(sizes, swap)
    sides = []
    for name, bit in steps:
        side = (lax.axis_index(name) // bit) % 2
        sides.append(side)
        pairs = [(at, at ^ bit) for at in range(sizes[name])]
        halves = block.reshape((2, block.shape[0] // 2) + block.shape[1:])
        kept = lax.dynamic_index_in_dim(halves, side, 0, keepdims=False)
        sent = lax.dynamic_index_in_dim(halves, 1 - side, 0, keepdims=False)
        received = lax.ppermute(sent, name, pairs)
        block = (kept.astype(F32) + received.astype(F32)).astype(BF16)
    for (name, bit), side in zip(reversed(steps), reversed(sides)):
        pairs = [(at, at ^ bit) for at in range(sizes[name])]
        received = lax.ppermute(block, name, pairs)
        block = jnp.where(side == 0, jnp.stack([block, received]), jnp.stack([received, block]))
        block = block.reshape((-1,) + block.shape[2:])
    return block


def sum_two_ways(block, sizes):
    half = block.shape[0] // 2
    return jnp.concatenate(
        [sum_everywhere(block[:half], sizes, False), sum_everywhere(block[half:], sizes, True)], axis=0
    )


def padded(rows, total):
    return jnp.pad(rows, ((0, total - rows.shape[0]), (0, 0)))


def on_device(
    sizes,
    tokens,
    cotangent,
    expert_ids,
    expert_slots,
    w_qkv,
    q_bias,
    v_bias,
    w_proj,
    proj_bias,
    gain_one,
    shift_one,
    gain_two,
    shift_two,
    w_router,
    expert_in,
    expert_in_bias,
    expert_out,
    expert_out_bias,
):
    row_count, width = tokens.shape
    experts = w_router.shape[1]
    slot_count = row_count // experts
    reps = sizes["rep"]
    gain_one, shift_one, gain_two, shift_two = (
        row[None] for row in (gain_one, shift_one, gain_two, shift_two)
    )
    bias = jnp.concatenate([q_bias.astype(F32), jnp.zeros((width,), F32), v_bias.astype(F32)])[None]
    columns = jnp.where(expert_slots >= 0, expert_ids * slot_count + expert_slots, -1)
    turned = columns.T
    weight_in = expert_in[0]
    weight_out = expert_out[0]
    bias_in = expert_in_bias.astype(F32)
    bias_out = expert_out_bias.astype(F32)

    cot_arrived = exchange(gather(turned, cotangent), experts)
    normed_one, qkv, weights, inverse, context, residual, normed_two, router = front(
        tokens,
        w_qkv,
        bias,
        w_proj,
        proj_bias.astype(F32)[None],
        gain_one,
        shift_one,
        gain_two,
        shift_two,
        w_router,
    )
    arrived = exchange(dispatch(turned, normed_two, router, slot_count), experts)
    raw = raw_active(cot_arrived, weight_out)
    active, grad_hidden, out_grad, in_bias_grad, out_bias_grad, back = expert(
        arrived, cot_arrived, weight_in, bias_in, raw, bias_out
    )
    grad_eout = lax.psum_scatter(out_grad, "rep", scatter_dimension=0, tiled=True)
    source = exchange(back, experts)
    part = weight_in.shape[1] // reps
    out_part = width // reps
    tail = jnp.pad(out_bias_grad.reshape(reps, 1, out_part), ((0, 0), (0, 0), (0, part - out_part)))
    in_grad = weight_in_grad(arrived, grad_hidden, in_bias_grad, tail, width, reps)
    packed_in = lax.psum_scatter(
        in_grad.reshape(reps * (width + 16), part), "rep", scatter_dimension=0, tiled=True
    )
    returned = exchange(produce(arrived, active, weight_out, bias_out), experts)
    grad_residual, grad_context, proj_grad, vectors_two, router_grad = middle(
        columns, source, router, normed_two, residual, cotangent, context, w_router, w_proj, gain_two, slot_count
    )
    grain = 2 * 16 * sizes["rep"] * sizes["exp"]
    early = jnp.concatenate([proj_grad, vectors_two.astype(BF16), router_grad.astype(BF16)], axis=0)
    early = sum_two_ways(padded(early, -(-early.shape[0] // grain) * grain), sizes)
    grad_qkv, qkv_grad = attend_back(
        grad_context, qkv, weights, inverse, context, normed_one, 0, width // PAIR
    )
    mixed = combine(columns, returned, residual)
    grad_tokens, vectors_one = last(tokens, grad_qkv, w_qkv, grad_residual, gain_one)
    late = jnp.concatenate([qkv_grad.reshape(3 * width, width), vectors_one.astype(BF16)], axis=0)
    late = sum_two_ways(padded(late, -(-late.shape[0] // grain) * grain), sizes)
    grad_w_qkv = jnp.transpose(late[: 3 * width].reshape(3, width, width), (1, 0, 2)).reshape(width, 3 * width)
    vectors_one = late[3 * width : 3 * width + 8].astype(F32)
    vectors_two = early[width : width + 8].astype(F32)
    return (
        mixed,
        grad_tokens,
        grad_w_qkv.astype(F32),
        vectors_one[2],
        vectors_one[3],
        early[:width].astype(F32),
        vectors_two[2],
        vectors_one[0],
        vectors_one[1],
        vectors_two[0],
        vectors_two[1],
        early[width + 8 : width + 8 + experts].astype(F32).T,
        packed_in[None, :width].astype(F32),
        packed_in[width : width + 1].astype(F32),
        grad_eout[None].astype(F32),
        packed_in[width + 1 : width + 2, :out_part].astype(F32),
    )


def solution(mesh):
    rows = P(("rep", "exp"), None)
    placed = (rows,) * 4 + (P(),) * 10 + (
        P("exp", None, None),
        P("exp", None),
        P("exp", None, None),
        P("exp", None),
    )
    return jax.shard_map(
        functools.partial(on_device, dict(mesh.shape)),
        mesh=mesh,
        in_specs=placed,
        out_specs=(rows, rows)
        + (P(),) * 10
        + (P("exp", None, "rep"), P("exp", "rep"), P("exp", "rep", None), P("exp", "rep")),
        check_vma=False,
    )
```

time: 728 us -> 427 us (0.59)
  the two profiles are of different devices: /device:TPU:0 before, /device:TPU:27 now
where the time goes in v1:
time: 427 us; the launch traced here: 419 us
  Pallas kernels  193 us (45%)
  waiting for transfers between devices  107 us (25%)
  starting transfers between devices  46.4 us (11%)
  local copies, waits for them, and re-layouts  30.5 us (7%)
  other arithmetic  27.8 us (7%)
  between operations  15 us (4%)
    ppermute x20, waiting for transfers between devices, sum_everywhere(): received = lax.ppermute(sent, name, pairs)  62.7 us
    pallas_call x1, Pallas kernels, front(): pl.pallas_call(functools.partial(front_kernel, SEQ // 2), grid=(images, p...  36 us
    pallas_call x1, Pallas kernels, attend_back(): pl.pallas_call(functools.partial(attend_back_kernel, SEQ), grid=(count, i...  32.5 us
    pallas_call x1, Pallas kernels, expert(): pl.pallas_call(functools.partial(expert_kernel, 288), grid=(hidden // chu...  32.1 us
    pallas_call x1, Pallas kernels, middle(): pl.pallas_call(functools.partial(middle_kernel, slot_count), grid=(images...  28.8 us
    ppermute x20, waiting for transfers between devices, sum_everywhere(): received = lax.ppermute(block, name, pairs)  28.7 us
    all_to_all x4, starting transfers between devices, exchange(): lax.all_to_all(blocks, 'exp', split_axis=0, concat_axis=0, tiled=True)  20 us
    ppermute x20, starting transfers between devices, sum_everywhere(): received = lax.ppermute(block, name, pairs)  17.9 us
  transfers between devices with their start and end apart: 46, of which 26 were waited for; matrix products, arithmetic and copies ran while one was open for 11% of the time, Pallas kernels for 37%

profile of v1, /device:TPU:27, one launch (start us, length us, event | category | flops | bytes accessed | tf_op | source)
XLA Modules:
  0.0 419.2 jit_solution(8784054954751262425)
XLA Ops:
  11.1 5.5 %gather.1 = bf16[1152,768]{1,0:T(8,128)(2,1)} custom-call(s32[2,1152]{1,0:T(2,128)} %copy.56.columns, bf16[1152,768]{1,0:T(8,128)(2,1)} %cotangent.1), custom_call_target="tpu_custom_call" | custom-call | tf_op jit(solution)/shard_map/gather/pallas_call | solution.py:227
  16.6 4.7 %all-to-all-start.1 = ((bf16[8,144,768]{2,1,0:T(8,128)(2,1)}), bf16[8,144,768]{2,1,0:T(8,128)(2,1)S(1)}, u32[]{:S(2)}, u32[]{:S(2)}) async-start(bf16[8,144,768]{2,1,0:T(8,128)(2,1)} %bitcast.227), calls=%async_computation.1 | async-start | bytes 3538944 | tf_op jit(solution)/shard_map/all_to_all | solution.py:726
  25.8 36.0 %front.1 = (bf16[1152,768]{1,0:T(8,128)(2,1)}, bf16[2,18,576,128]{3,2,1,0:T(8,128)(2,1)}, bf16[2,6,576,1152]{3,2,1,0:T(8,128)(2,1)}, f32[2,6,576,128]{3,2,1,0:T(...) custom-call(bf16[1152,768]{1,0:T(8,128)(2,1)} %tokens.3, ...), custom_call_target="tpu_custom_call" | custom-call | tf_op jit(solution)/shard_map/front/pallas_call | solution.py:184
  61.8 7.9 %dispatch.1 = bf16[1152,896]{1,0:T(8,128)(2,1)} custom-call(s32[2,1152]{1,0:T(2,128)} %copy.56.columns, bf16[1152,768]{1,0:T(8,128)(2,1)} %get-tuple-element.39.rows.normed_two, f32[1152,8]{1,0:T(8,128)} %get-tuple-element.40.router), custom_call_target="tpu_custom_call" | custom-call | tf_op jit(solution)/shard_map/dispatch/pallas_call | solution.py:265
  70.9 4.2 %all-to-all-start = ((bf16[8,144,896]{2,1,0:T(8,128)(2,1)}), bf16[8,144,896]{2,1,0:T(8,128)(2,1)S(1)}, u32[]{:S(2)}, u32[]{:S(2)}) async-start(bf16[8,144,896]{2,1,0:T(8,128)(2,1)} %bitcast.226), calls=%async_computation | async-start | bytes 4128768 | tf_op jit(solution)/shard_map/all_to_all | solution.py:726
  76.6 10.5 %raw_active.1.raw = bf16[1152,3072]{1,0:T(8,128)(2,1)} custom-call(bf16[1152,768]{1,0:T(8,128)(2,1)} %bitcast.215, bf16[3072,768]{1,0:T(8,128)(2,1)} %bitcast.213), custom_call_target="tpu_custom_call" | custom-call | tf_op jit(solution)/shard_map/raw_active/pallas_call | solution.py:283
  87.1 12.8 %all-to-all-done = bf16[8,144,896]{2,1,0:T(8,128)(2,1)S(1)} async-done(((bf16[8,144,896]{2,1,0:T(8,128)(2,1)}), bf16[8,144,896]{2,1,0:T(8,128)(2,1)S(1)}, u32[]{:S(2)}, u32[]{:S(2)}) %all-to-all-start) | async-done | bytes 2064416 | tf_op jit(solution)/shard_map/all_to_all | solution.py:726
  101.2 32.1 %expert.1 = (bf16[1152,3072]{1,0:T(8,128)(2,1)}, bf16[1152,3072]{1,0:T(8,128)(2,1)}, bf16[3072,768]{1,0:T(8,128)(2,1)}, f32[1,3072]{1,0:T(1,128)}, f32[1,768]{1,0:T(1,128)}, /*index=5*/bf16[1152,896]{1,0:T(8,128)(2,1)}) custom-call(bf16[1152,896]{1,0:T(8,128)(2,1)} %bitcast.208, bf16[1152,768]{1,0:T(8,128)(2,1)} %bitcast.216, bf16[768,3072]{1,0:T(8,128)(2,1)} %bitcast.235, ...), custom_call_target="tpu_custom_call" | custom-call | tf_op jit(solution)/shard_map/expert/pallas_call | solution.py:357
  133.3 5.1 %all-to-all-start.3 = ((bf16[8,144,896]{2,1,0:T(8,128)(2,1)}), bf16[8,144,896]{2,1,0:T(8,128)(2,1)S(1)}, u32[]{:S(2)}, u32[]{:S(2)}) async-start(bf16[8,144,896]{2,1,0:T(8,128)(2,1)} %bitcast.251), calls=%async_computation.3 | async-start | bytes 4128768 | tf_op jit(solution)/shard_map/all_to_all | solution.py:726
  138.4 11.0 %produce.1 = bf16[1152,768]{1,0:T(8,128)(2,1)} custom-call(bf16[1152,896]{1,0:T(8,128)(2,1)} %bitcast.209, bf16[1152,3072]{1,0:T(8,128)(2,1)} %get-tuple-element.41.active, bf16[3072,768]{1,0:T(8,128)(2,1)} %bitcast.214, f32[1,768]{1,0:T(1,128)} %convert_element_type.311.bias_out), custom_call_target="tpu_custom_call" | custom-call | tf_op jit(solution)/shard_map/produce/pallas_call | solution.py:434
  150.1 10.8 %weight_in_grad.1 = bf16[4,784,768]{2,1,0:T(8,128)(2,1)} custom-call(bf16[1152,896]{1,0:T(8,128)(2,1)} %bitcast.210, bf16[1152,3072]{1,0:T(8,128)(2,1)} %get-tuple-element.58.grad_hidden, f32[1,3072]{1,0:T(1,128)} %get-tuple-element.59.bias_grad, f32[4,1,768]{2,1,0:T(1,128)} %pad.14.out_bias_grad), custom_call_target="tpu_custom_call" | custom-call | tf_op jit(solution)/shard_map/weight_in_grad/pallas_call | solution.py:409
  163.2 6.0 %all-to-all-start.2 = ((bf16[8,144,768]{2,1,0:T(8,128)(2,1)}), bf16[8,144,768]{2,1,0:T(8,128)(2,1)}, u32[]{:S(2)}, u32[]{:S(2)}) async-start(bf16[8,144,768]{2,1,0:T(8,128)(2,1)} %bitcast.228), calls=%async_computation.2 | async-start | bytes 3538944 | tf_op jit(solution)/shard_map/all_to_all | solution.py:726
  169.3 28.8 %middle.1 = (f32[1152,768]{1,0:T(8,128)}, bf16[2,6,576,128]{3,2,1,0:T(8,128)(2,1)}, bf16[768,768]{1,0:T(8,128)(2,1)}, f32[8,768]{1,0:T(8,128)}, f32[8,768]{1,0:T(8,128)}) custom-call(s32[1152,2]{1,0:T(8,128)} %copy-done.3, bf16[1152,896]{1,0:T(8,128)(2,1)} %bitcast.225, f32[1152,8]{1,0:T(8,128)} %get-tuple-element.40.router, ...), custom_call_target="tpu_custom_call" | custom-call | tf_op jit(solution)/shard_map/middle/pallas_call | solution.py:529
  198.1 32.5 %attend_back.1 = (bf16[3,6,1152,128]{3,2,1,0:T(8,128)(2,1)}, bf16[3,768,768]{2,1,0:T(8,128)(2,1)}) custom-call(bf16[2,6,576,128]{3,2,1,0:T(8,128)(2,1)} %get-tuple-element.45.grad_context, bf16[2,18,576,128]{3,2,1,0:T(8,128)(2,1)} %get-tuple-element.46.queries.keys.values, bf16[2,18,576,128]{3,2,1,0:T(8,128)(2,1)} %get-tuple-element.46.queries.keys.values, ...), custom_call_target="tpu_custom_call" | custom-call | tf_op jit(solution)/shard_map/attend_back/pallas_call | solution.py:635
  230.6 11.2 %last.1 = (f32[1152,768]{1,0:T(8,128)}, f32[8,768]{1,0:T(8,128)}) custom-call(bf16[1152,768]{1,0:T(8,128)(2,1)} %tokens.3, bf16[3,6,1152,128]{3,2,1,0:T(8,128)(2,1)} %get-tuple-element.50.grad_qkv, bf16[768,2304]{1,0:T(8,128)(2,1)} %w_qkv.3, f32[1152,768]{1,0:T(8,128)} %get-tuple-element.51.grad_residual, f32[1,768]{1,0:T(1,128)} %broadcast_in_dim.34.gain_one), custom_call_target="tpu_custom_call" | custom-call | tf_op jit(solution)/shard_map/last/pallas_call | solution.py:685
  248.5 3.8 collective-permute-done.31
  259.1 4.5 %collective-permute-done.33 = bf16[32,768]{1,0:T(8,128)(2,1)S(1)} collective-permute-done((bf16[32,768]{1,0:T(8,128)(2,1)S(1)}, bf16[32,768]{1,0:T(8,128)(2,1)S(1)}, u32[]{:S(2)}, u32[]{:S(2)}) %collective-permute-start.33) | collective-permute-done | bytes 49184 | tf_op jit(solution)/shard_map/ppermute | solution.py:753
  266.1 5.9 %collective-permute-done.34 = bf16[16,768]{1,0:T(8,128)(2,1)S(1)} collective-permute-done((bf16[16,768]{1,0:T(8,128)(2,1)S(1)}, bf16[16,768]{1,0:T(8,128)(2,1)S(1)}, u32[]{:S(2)}, u32[]{:S(2)}) %collective-permute-start.34) | collective-permute-done | bytes 24608 | tf_op jit(solution)/shard_map/ppermute | solution.py:753
  277.0 10.3 %collective-permute-done.11 = bf16[384,768]{1,0:T(8,128)(2,1)S(1)} collective-permute-done((bf16[384,768]{1,0:T(8,128)(2,1)S(1)}, bf16[384,768]{1,0:T(8,128)(2,1)S(1)}, u32[]{:S(2)}, u32[]{:S(2)}) %collective-permute-start.11) | collective-permute-done | bytes 589856 | tf_op jit(solution)/shard_map/ppermute | solution.py:753
  289.2 5.8 %collective-permute-done.12 = bf16[192,768]{1,0:T(8,128)(2,1)S(1)} collective-permute-done((bf16[192,768]{1,0:T(8,128)(2,1)S(1)}, bf16[192,768]{1,0:T(8,128)(2,1)S(1)}, u32[]{:S(2)}, u32[]{:S(2)}) %collective-permute-start.12) | collective-permute-done | bytes 294944 | tf_op jit(solution)/shard_map/ppermute | solution.py:753
  296.8 8.9 %collective-permute-done.13 = bf16[96,768]{1,0:T(8,128)(2,1)S(1)} collective-permute-done((bf16[96,768]{1,0:T(8,128)(2,1)S(1)}, bf16[96,768]{1,0:T(8,128)(2,1)S(1)}, u32[]{:S(2)}, u32[]{:S(2)}) %collective-permute-start.13) | collective-permute-done | bytes 147488 | tf_op jit(solution)/shard_map/ppermute | solution.py:753
  305.8 7.6 %collective-permute-done.3 = bf16[96,768]{1,0:T(8,128)(2,1)S(1)} collective-permute-done((bf16[96,768]{1,0:T(8,128)(2,1)S(1)}, bf16[96,768]{1,0:T(8,128)(2,1)S(1)}, u32[]{:S(2)}, u32[]{:S(2)}) %collective-permute-start.3) | collective-permute-done | bytes 147488 | tf_op jit(solution)/shard_map/ppermute | solution.py:753
  316.1 6.6 %collective-permute-done.4 = bf16[48,768]{1,0:T(8,128)(2,1)S(1)} collective-permute-done((bf16[48,768]{1,0:T(8,128)(2,1)S(1)}, bf16[48,768]{1,0:T(8,128)(2,1)S(1)}, u32[]{:S(2)}, u32[]{:S(2)}) %collective-permute-start.4) | collective-permute-done | bytes 73760 | tf_op jit(solution)/shard_map/ppermute | solution.py:753
  322.7 3.1 collective-permute-done.15
  331.1 3.0 collective-permute-done.6
  342.0 12.9 %collective-permute-done.27 = bf16[64,768]{1,0:T(8,128)(2,1)S(1)} collective-permute-done((bf16[64,768]{1,0:T(8,128)(2,1)S(1)}, bf16[64,768]{1,0:T(8,128)(2,1)S(1)}, u32[]{:S(2)}, u32[]{:S(2)}) %collective-permute-start.27) | collective-permute-done | bytes 98336 | tf_op jit(solution)/shard_map/ppermute | solution.py:757
  355.0 4.1 collective-permute-done.38
  359.2 3.5 collective-permute-start.39
  366.4 6.7 %combine.1 = bf16[1152,768]{1,0:T(8,128)(2,1)} custom-call(s32[1152,2]{1,0:T(8,128)} %copy-done.3, bf16[1152,768]{1,0:T(8,128)(2,1)} %bitcast.8.source, f32[1152,768]{1,0:T(8,128)} %get-tuple-element.42.residual), custom_call_target="tpu_custom_call" | custom-call | tf_op jit(solution)/shard_map/combine/pallas_call | solution.py:709
  382.8 3.6 convert_bitcast_fusion
  386.4 8.0 %copy.58 = f32[768,3,768]{0,2,1:T(8,128)} copy(f32[768,3,768]{2,0,1:T(8,128)} %convert_bitcast_fusion) | data formatting | bytes 14155776 | tf_op jit(solution)/shard_map/convert_element_type | solution.py:857
  394.4 8.0 %copy.59 = f32[768,2304]{1,0:T(8,128)} copy(f32[768,2304]{0,1:T(8,128)} %bitcast.211) | data formatting | bytes 14155776
  (214 shorter events, 79.0 us)
Async XLA Ops:
  16.6 53.1 %all-to-all-start.1 = ((bf16[8,144,768]{2,1,0:T(8,128)(2,1)}), bf16[8,144,768]{2,1,0:T(8,128)(2,1)S(1)}, u32[]{:S(2)}, u32[]{:S(2)}) async-start(bf16[8,144,768]{2,1,0:T(8,128)(2,1)} %bitcast.227), calls=%async_computation.1 | async-start | bytes 3538944 | tf_op jit(solution)/shard_map/all_to_all | solution.py:726
  70.9 28.9 %all-to-all-start = ((bf16[8,144,896]{2,1,0:T(8,128)(2,1)}), bf16[8,144,896]{2,1,0:T(8,128)(2,1)S(1)}, u32[]{:S(2)}, u32[]{:S(2)}) async-start(bf16[8,144,896]{2,1,0:T(8,128)(2,1)} %bitcast.226), calls=%async_computation | async-start | bytes 4128768 | tf_op jit(solution)/shard_map/all_to_all | solution.py:726
  75.1 328.8 %reduce-scatter.5.cloned.1.call-start = ((), (), s32[]{:S(2)}) async-start(), calls=%async_computation.7 | async-start | bytes 5898240 | tf_op jit(solution)/shard_map/reduce_scatter | solution.py:828
  133.3 30.0 %all-to-all-start.3 = ((bf16[8,144,896]{2,1,0:T(8,128)(2,1)}), bf16[8,144,896]{2,1,0:T(8,128)(2,1)S(1)}, u32[]{:S(2)}, u32[]{:S(2)}) async-start(bf16[8,144,896]{2,1,0:T(8,128)(2,1)} %bitcast.251), calls=%async_computation.3 | async-start | bytes 4128768 | tf_op jit(solution)/shard_map/all_to_all | solution.py:726
  138.4 268.4 %reduce-scatter.3.cloned.1.call-start = ((), (), s32[]{:S(2)}) async-start(), calls=%async_computation.6 | async-start | bytes 6021120 | tf_op jit(solution)/shard_map/reduce_scatter | solution.py:834
  163.2 203.1 %all-to-all-start.2 = ((bf16[8,144,768]{2,1,0:T(8,128)(2,1)}), bf16[8,144,768]{2,1,0:T(8,128)(2,1)}, u32[]{:S(2)}, u32[]{:S(2)}) async-start(bf16[8,144,768]{2,1,0:T(8,128)(2,1)} %bitcast.228), calls=%async_computation.2 | async-start | bytes 3538944 | tf_op jit(solution)/shard_map/all_to_all | solution.py:726
  244.8 27.3 %collective-permute-start.10 = (bf16[768,768]{1,0:T(8,128)(2,1)S(1)}, bf16[768,768]{1,0:T(8,128)(2,1)S(1)}, u32[]{:S(2)}, u32[]{:S(2)}) collective-permute-start(bf16[768,768]{1,0:T(8,128)(2,1)S(1)} %dynamic-slice_bitcast_fusion), channel_id=1, source_target_pairs={{0,1},{1,0},{2,3},{3,2},{4,5},{5,4},{6,7},{7,6},{8,9},{9,8},{10,11... | collective-permute-start | bytes 3538952 | tf_op jit(solution)/shard_map/ppermute | solution.py:753
  245.5 28.2 %collective-permute-start = (bf16[768,768]{1,0:T(8,128)(2,1)S(1)}, bf16[768,768]{1,0:T(8,128)(2,1)S(1)}, u32[]{:S(2)}, u32[]{:S(2)}) collective-permute-start(bf16[768,768]{1,0:T(8,128)(2,1)S(1)} %dynamic-slice_bitcast_fusion.1), channel_id=1, source_target_pairs={{0,1},{1,0},{2,3},{3,2},{4,5},{5,4},{6,7},{7,6},{8,9},{9,8},{10,11... | collective-permute-start | bytes 3538952 | tf_op jit(solution)/shard_map/ppermute | solution.py:753
  256.6 6.9 %collective-permute-start.33 = (bf16[32,768]{1,0:T(8,128)(2,1)S(1)}, bf16[32,768]{1,0:T(8,128)(2,1)S(1)}, u32[]{:S(2)}, u32[]{:S(2)}) collective-permute-start(bf16[32,768]{1,0:T(8,128)(2,1)S(1)} %dynamic-slice_bitcast_fusion.16), channel_id=1, source_target_pairs={{0,8},{8,0},{16,24},{24,16},{1,9},{9,1},{17,25},{25,17},{2,10},{10... | collective-permute-start | bytes 147464 | tf_op jit(solution)/shard_map/ppermute | solution.py:753
  263.6 8.4 %collective-permute-start.34 = (bf16[16,768]{1,0:T(8,128)(2,1)S(1)}, bf16[16,768]{1,0:T(8,128)(2,1)S(1)}, u32[]{:S(2)}, u32[]{:S(2)}) collective-permute-start(bf16[16,768]{1,0:T(8,128)(2,1)S(1)} %dynamic-slice_bitcast_fusion.18), channel_id=1, source_target_pairs={{0,16},{8,24},{16,0},{24,8},{1,17},{9,25},{17,1},{25,9},{2,18},{10... | collective-permute-start | bytes 73736 | tf_op jit(solution)/shard_map/ppermute | solution.py:753
  265.6 9.0 %collective-permute-start.24 = (bf16[16,768]{1,0:T(8,128)(2,1)S(1)}, bf16[16,768]{1,0:T(8,128)(2,1)S(1)}, u32[]{:S(2)}, u32[]{:S(2)}) collective-permute-start(bf16[16,768]{1,0:T(8,128)(2,1)S(1)} %dynamic-slice_bitcast_fusion.19), channel_id=1, source_target_pairs={{0,16},{8,24},{16,0},{24,8},{1,17},{9,25},{17,1},{25,9},{2,18},{10... | collective-permute-start | bytes 73736 | tf_op jit(solution)/shard_map/ppermute | solution.py:753
  272.0 55.6 %collective-permute-start.35 = (bf16[16,768]{1,0:T(8,128)(2,1)S(1)}, bf16[16,768]{1,0:T(8,128)(2,1)S(1)}, u32[]{:S(2)}, u32[]{:S(2)}) collective-permute-start(bf16[16,768]{1,0:T(8,128)(2,1)S(1)} %fusion.28), channel_id=1, source_target_pairs={{0,16},{8,24},{16,0},{24,8},{1,17},{9,25},{17,1},{25,9},{2,18},{10... | collective-permute-start | bytes 73736 | tf_op jit(solution)/shard_map/ppermute | solution.py:757
  272.5 14.7 %collective-permute-start.11 = (bf16[384,768]{1,0:T(8,128)(2,1)S(1)}, bf16[384,768]{1,0:T(8,128)(2,1)S(1)}, u32[]{:S(2)}, u32[]{:S(2)}) collective-permute-start(bf16[384,768]{1,0:T(8,128)(2,1)S(1)} %dynamic-slice_bitcast_fusion.2), channel_id=1, source_target_pairs={{0,4},{1,5},{2,6},{3,7},{4,0},{5,1},{6,2},{7,3},{8,12},{9,13},{10,... | collective-permute-start | bytes 1769480 | tf_op jit(solution)/shard_map/ppermute | solution.py:753
  274.2 14.4 %collective-permute-start.1 = (bf16[384,768]{1,0:T(8,128)(2,1)S(1)}, bf16[384,768]{1,0:T(8,128)(2,1)S(1)}, u32[]{:S(2)}, u32[]{:S(2)}) collective-permute-start(bf16[384,768]{1,0:T(8,128)(2,1)S(1)} %dynamic-slice_bitcast_fusion.3), channel_id=1, source_target_pairs={{0,2},{1,3},{2,0},{3,1},{4,6},{5,7},{6,4},{7,5},{8,10},{9,11},{10,... | collective-permute-start | bytes 1769480 | tf_op jit(solution)/shard_map/ppermute | solution.py:753
  274.5 60.7 %collective-permute-start.25 = (bf16[16,768]{1,0:T(8,128)(2,1)S(1)}, bf16[16,768]{1,0:T(8,128)(2,1)S(1)}, u32[]{:S(2)}, u32[]{:S(2)}) collective-permute-start(bf16[16,768]{1,0:T(8,128)(2,1)S(1)} %fusion.29), channel_id=1, source_target_pairs={{0,16},{8,24},{16,0},{24,8},{1,17},{9,25},{17,1},{25,9},{2,18},{10... | collective-permute-start | bytes 73736 | tf_op jit(solution)/shard_map/ppermute | solution.py:757
  287.4 7.5 %collective-permute-start.12 = (bf16[192,768]{1,0:T(8,128)(2,1)S(1)}, bf16[192,768]{1,0:T(8,128)(2,1)S(1)}, u32[]{:S(2)}, u32[]{:S(2)}) collective-permute-start(bf16[192,768]{1,0:T(8,128)(2,1)S(1)} %dynamic-slice_bitcast_fusion.6), channel_id=1, source_target_pairs={{0,2},{1,3},{2,0},{3,1},{4,6},{5,7},{6,4},{7,5},{8,10},{9,11},{10,... | collective-permute-start | bytes 884744 | tf_op jit(solution)/shard_map/ppermute | solution.py:753
  288.8 7.2 %collective-permute-start.2 = (bf16[192,768]{1,0:T(8,128)(2,1)S(1)}, bf16[192,768]{1,0:T(8,128)(2,1)S(1)}, u32[]{:S(2)}, u32[]{:S(2)}) collective-permute-start(bf16[192,768]{1,0:T(8,128)(2,1)S(1)} %dynamic-slice_bitcast_fusion.7), channel_id=1, source_target_pairs={{0,4},{1,5},{2,6},{3,7},{4,0},{5,1},{6,2},{7,3},{8,12},{9,13},{10,... | collective-permute-start | bytes 884744 | tf_op jit(solution)/shard_map/ppermute | solution.py:753
  295.1 10.6 %collective-permute-start.13 = (bf16[96,768]{1,0:T(8,128)(2,1)S(1)}, bf16[96,768]{1,0:T(8,128)(2,1)S(1)}, u32[]{:S(2)}, u32[]{:S(2)}) collective-permute-start(bf16[96,768]{1,0:T(8,128)(2,1)S(1)} %dynamic-slice_bitcast_fusion.10), channel_id=1, source_target_pairs={{0,8},{8,0},{16,24},{24,16},{1,9},{9,1},{17,25},{25,17},{2,10},{10... | collective-permute-start | bytes 442376 | tf_op jit(solution)/shard_map/ppermute | solution.py:753
  296.1 17.4 %collective-permute-start.3 = (bf16[96,768]{1,0:T(8,128)(2,1)S(1)}, bf16[96,768]{1,0:T(8,128)(2,1)S(1)}, u32[]{:S(2)}, u32[]{:S(2)}) collective-permute-start(bf16[96,768]{1,0:T(8,128)(2,1)S(1)} %dynamic-slice_bitcast_fusion.11), channel_id=1, source_target_pairs={{0,8},{8,0},{16,24},{24,16},{1,9},{9,1},{17,25},{25,17},{2,10},{10... | collective-permute-start | bytes 442376 | tf_op jit(solution)/shard_map/ppermute | solution.py:753
  305.7 7.9 %collective-permute-start.14 = (bf16[48,768]{1,0:T(8,128)(2,1)S(1)}, bf16[48,768]{1,0:T(8,128)(2,1)S(1)}, u32[]{:S(2)}, u32[]{:S(2)}) collective-permute-start(bf16[48,768]{1,0:T(8,128)(2,1)S(1)} %dynamic-slice_bitcast_fusion.14), channel_id=1, source_target_pairs={{0,16},{8,24},{16,0},{24,8},{1,17},{9,25},{17,1},{25,9},{2,18},{10... | collective-permute-start | bytes 221192 | tf_op jit(solution)/shard_map/ppermute | solution.py:753
  313.5 9.1 %collective-permute-start.4 = (bf16[48,768]{1,0:T(8,128)(2,1)S(1)}, bf16[48,768]{1,0:T(8,128)(2,1)S(1)}, u32[]{:S(2)}, u32[]{:S(2)}) collective-permute-start(bf16[48,768]{1,0:T(8,128)(2,1)S(1)} %dynamic-slice_bitcast_fusion.15), channel_id=1, source_target_pairs={{0,16},{8,24},{16,0},{24,8},{1,17},{9,25},{17,1},{25,9},{2,18},{10... | collective-permute-start | bytes 221192 | tf_op jit(solution)/shard_map/ppermute | solution.py:753
  313.7 12.1 %collective-permute-start.15 = (bf16[48,768]{1,0:T(8,128)(2,1)S(1)}, bf16[48,768]{1,0:T(8,128)(2,1)S(1)}, u32[]{:S(2)}, u32[]{:S(2)}) collective-permute-start(bf16[48,768]{1,0:T(8,128)(2,1)S(1)} %fusion.24), channel_id=1, source_target_pairs={{0,16},{8,24},{16,0},{24,8},{1,17},{9,25},{17,1},{25,9},{2,18},{10... | collective-permute-start | bytes 221192 | tf_op jit(solution)/shard_map/ppermute | solution.py:757
  327.6 7.7 %collective-permute-start.36 = (bf16[32,768]{1,0:T(8,128)(2,1)S(1)}, bf16[32,768]{1,0:T(8,128)(2,1)S(1)}, u32[]{:S(2)}, u32[]{:S(2)}) collective-permute-start(bf16[32,768]{1,0:T(8,128)(2,1)S(1)} %bitcast.302), channel_id=1, source_target_pairs={{0,8},{8,0},{16,24},{24,16},{1,9},{9,1},{17,25},{25,17},{2,10},{10... | collective-permute-start | bytes 147464 | tf_op jit(solution)/shard_map/ppermute | solution.py:757
  336.2 26.5 %collective-permute-start.18 = (bf16[384,768]{1,0:T(8,128)(2,1)S(1)}, bf16[384,768]{1,0:T(8,128)(2,1)S(1)}, u32[]{:S(2)}, u32[]{:S(2)}) collective-permute-start(bf16[384,768]{1,0:T(8,128)(2,1)S(1)} %bitcast.243), channel_id=1, source_target_pairs={{0,4},{1,5},{2,6},{3,7},{4,0},{5,1},{6,2},{7,3},{8,12},{9,13},{10,... | collective-permute-start | bytes 1769480 | tf_op jit(solution)/shard_map/ppermute | solution.py:757
  340.2 22.7 %collective-permute-start.8 = (bf16[384,768]{1,0:T(8,128)(2,1)S(1)}, bf16[384,768]{1,0:T(8,128)(2,1)S(1)}, u32[]{:S(2)}, u32[]{:S(2)}) collective-permute-start(bf16[384,768]{1,0:T(8,128)(2,1)S(1)} %bitcast.245), channel_id=1, source_target_pairs={{0,2},{1,3},{2,0},{3,1},{4,6},{5,7},{6,4},{7,5},{8,10},{9,11},{10,... | collective-permute-start | bytes 1769480 | tf_op jit(solution)/shard_map/ppermute | solution.py:757
  340.4 14.5 %collective-permute-start.27 = (bf16[64,768]{1,0:T(8,128)(2,1)S(1)}, bf16[64,768]{1,0:T(8,128)(2,1)S(1)}, u32[]{:S(2)}, u32[]{:S(2)}) collective-permute-start(bf16[64,768]{1,0:T(8,128)(2,1)S(1)} %bitcast.289), channel_id=1, source_target_pairs={{0,4},{1,5},{2,6},{3,7},{4,0},{5,1},{6,2},{7,3},{8,12},{9,13},{10,... | collective-permute-start | bytes 294920 | tf_op jit(solution)/shard_map/ppermute | solution.py:757
  341.9 17.2 %collective-permute-start.38 = (bf16[128,768]{1,0:T(8,128)(2,1)S(1)}, bf16[128,768]{1,0:T(8,128)(2,1)S(1)}, u32[]{:S(2)}, u32[]{:S(2)}) collective-permute-start(bf16[128,768]{1,0:T(8,128)(2,1)S(1)} %bitcast.271), channel_id=1, source_target_pairs={{0,4},{1,5},{2,6},{3,7},{4,0},{5,1},{6,2},{7,3},{8,12},{9,13},{10,... | collective-permute-start | bytes 589832 | tf_op jit(solution)/shard_map/ppermute | solution.py:757
  354.9 9.8 %collective-permute-start.28 = (bf16[128,768]{1,0:T(8,128)(2,1)S(1)}, bf16[128,768]{1,0:T(8,128)(2,1)S(1)}, u32[]{:S(2)}, u32[]{:S(2)}) collective-permute-start(bf16[128,768]{1,0:T(8,128)(2,1)S(1)} %bitcast.269), channel_id=1, source_target_pairs={{0,2},{1,3},{2,0},{3,1},{4,6},{5,7},{6,4},{7,5},{8,10},{9,11},{10,... | collective-permute-start | bytes 589832 | tf_op jit(solution)/shard_map/ppermute | solution.py:757
  359.2 13.9 %collective-permute-start.39 = (bf16[256,768]{1,0:T(8,128)(2,1)S(1)}, bf16[256,768]{1,0:T(8,128)(2,1)}, u32[]{:S(2)}, u32[]{:S(2)}) collective-permute-start(bf16[256,768]{1,0:T(8,128)(2,1)S(1)} %bitcast.252), channel_id=1, source_target_pairs={{0,1},{1,0},{2,3},{3,2},{4,5},{5,4},{6,7},{7,6},{8,9},{9,8},{10,11... | collective-permute-start | bytes 1179656 | tf_op jit(solution)/shard_map/ppermute | solution.py:757
  362.9 13.7 %collective-permute-start.19 = (bf16[768,768]{1,0:T(8,128)(2,1)S(1)}, bf16[768,768]{1,0:T(8,128)(2,1)S(1)}, u32[]{:S(2)}, u32[]{:S(2)}) collective-permute-start(bf16[768,768]{1,0:T(8,128)(2,1)S(1)} %bitcast.229), channel_id=1, source_target_pairs={{0,1},{1,0},{2,3},{3,2},{4,5},{5,4},{6,7},{7,6},{8,9},{9,8},{10,11... | collective-permute-start | bytes 3538952 | tf_op jit(solution)/shard_map/ppermute | solution.py:757
  364.2 15.6 %collective-permute-start.9 = (bf16[768,768]{1,0:T(8,128)(2,1)}, bf16[768,768]{1,0:T(8,128)(2,1)}, u32[]{:S(2)}, u32[]{:S(2)}) collective-permute-start(bf16[768,768]{1,0:T(8,128)(2,1)} %bitcast.38), channel_id=1, source_target_pairs={{0,1},{1,0},{2,3},{3,2},{4,5},{5,4},{6,7},{7,6},{8,9},{9,8},{10,11... | collective-permute-start | bytes 3538952 | tf_op jit(solution)/shard_map/ppermute | solution.py:757
  364.7 9.5 %collective-permute-start.29 = (bf16[256,768]{1,0:T(8,128)(2,1)S(1)}, bf16[256,768]{1,0:T(8,128)(2,1)S(1)}, u32[]{:S(2)}, u32[]{:S(2)}) collective-permute-start(bf16[256,768]{1,0:T(8,128)(2,1)S(1)} %bitcast.254), channel_id=1, source_target_pairs={{0,1},{1,0},{2,3},{3,2},{4,5},{5,4},{6,7},{7,6},{8,9},{9,8},{10,11... | collective-permute-start | bytes 1179656 | tf_op jit(solution)/shard_map/ppermute | solution.py:757
  (34 other events, 176.3 us)
Sparse Core Ops, SparseCore 0:
  133.4 84.6 reduce-scatter.4
  220.4 100.2 reduce-scatter.2

commit v2 on v1

v2 whole, which is shorter than its diff:
```python
import functools

import jax
import jax.numpy as jnp
from jax import lax
from jax.experimental import pallas as pl
from jax.experimental.pallas import tpu as pltpu
from jax.sharding import PartitionSpec as P

HEAD_DIM = 64
SEQ = 576
PAIR = 2 * HEAD_DIM
SPLIT = 512
AUX = 128
EPSILON = 1e-06
F32 = jnp.float32
BF16 = jnp.bfloat16
VMEM_BYTES = 56 * 2**20


def dot(left, right):
    return lax.dot_general(left, right, (((1,), (0,)), ((), ())), preferred_element_type=F32)


def dot_last(left, right):
    return lax.dot_general(left, right, (((1,), (1,)), ((), ())), preferred_element_type=F32)


def dot_first(left, right):
    return lax.dot_general(left, right, (((0,), (0,)), ((), ())), preferred_element_type=F32)


def thirds(value):
    high = value.astype(BF16)
    rest = value - high.astype(F32)
    middle = rest.astype(BF16)
    return high, middle, (rest - middle.astype(F32)).astype(BF16)


def standardize(field):
    centred = field - jnp.mean(field, axis=-1, keepdims=True)
    inverse = lax.rsqrt(jnp.mean(centred * centred, axis=-1, keepdims=True) + EPSILON)
    return centred * inverse, inverse


def standardize_back(grad, gain, unit, inverse):
    scaled = grad * gain
    along = jnp.mean(scaled * unit, axis=-1, keepdims=True)
    return inverse * (scaled - jnp.mean(scaled, axis=-1, keepdims=True) - unit * along)


def as_row(ref):
    return ref[...].astype(F32).reshape(1, -1)


def column_sum(field):
    return jnp.sum(field, axis=0, keepdims=True)


def params():
    return pltpu.CompilerParams(vmem_limit_bytes=VMEM_BYTES)


SCALE = 0.01


def cost(flops, bytes_moved):
    return pl.CostEstimate(flops=int(flops * SCALE), transcendentals=0, bytes_accessed=int(bytes_moved * SCALE))


def whole(array):
    return pl.BlockSpec(array.shape, lambda *ids: (0,) * array.ndim)


def shape(dims, kind):
    return jax.ShapeDtypeStruct(dims, kind)


def split_heads(pair):
    lane = lax.broadcasted_iota(jnp.int32, pair.shape, 1)
    zero = jnp.zeros_like(pair)
    first = jnp.where(lane < HEAD_DIM, pair, zero)
    second = jnp.where(lane < HEAD_DIM, zero, pair)
    return jnp.concatenate([first[:SPLIT], second[:SPLIT], first[SPLIT:], second[SPLIT:]], axis=0)


def key_sides():
    row = lax.broadcasted_iota(jnp.int32, (2 * SEQ, PAIR), 0)
    lane = lax.broadcasted_iota(jnp.int32, (2 * SEQ, PAIR), 1)
    is_first = (row < SPLIT) | ((row >= 2 * SPLIT) & (row < SPLIT + SEQ))
    return is_first, lane


def front_kernel(
    chunk,
    tokens,
    w_qkv,
    q_bias,
    v_bias,
    w_proj,
    proj_bias,
    gain_one,
    shift_one,
    gain_two,
    shift_two,
    normed_one_out,
    qkv_out,
    weights_out,
    inverse_out,
    context_out,
    residual_out,
    normed_two_out,
    value_side,
):
    pair = pl.program_id(1)
    pairs = context_out.shape[1]

    @pl.when((pl.program_id(0) == 0) & (pair == 0))
    def _():
        is_first, lane = key_sides()
        value_side[:, PAIR:] = jnp.where(is_first == (lane < HEAD_DIM), 1.0, 0.0).astype(BF16)

    @pl.when(pair == 0)
    def _():
        unit, _ = standardize(tokens[...].astype(F32))
        normed = (unit * as_row(gain_one) + as_row(shift_one)).astype(BF16)
        normed_one_out[...] = normed
        width = w_qkv.shape[1]
        step = 2 * PAIR
        for at in range(0, width, step):
            part = dot(normed, w_qkv[:, at : at + step])
            third = width // 3
            if at < third:
                part = part + as_row(q_bias)[:, at : at + step]
            if at >= 2 * third:
                part = part + as_row(v_bias)[:, at - 2 * third : at - 2 * third + step]
            part = part.astype(BF16)
            if at < third:
                part = part * jnp.asarray(HEAD_DIM**-0.5, BF16)
            qkv_out[0, at // PAIR] = part[:, :PAIR]
            qkv_out[0, at // PAIR + 1] = part[:, PAIR:]

    keys = split_heads(qkv_out[0, pairs + pair])
    value_side[:, :PAIR] = split_heads(qkv_out[0, 2 * pairs + pair])
    values = value_side[...]
    low = lax.broadcasted_iota(jnp.int32, (chunk, PAIR), 1) < HEAD_DIM
    for at in range(0, SEQ, chunk):
        rows = slice(at, at + chunk)
        scores = dot_last(qkv_out[0, pair, rows], keys)
        first = scores[:, :SPLIT]
        second = scores[:, SPLIT : 2 * SPLIT]
        tail = scores[:, 2 * SPLIT :]
        first_max = jnp.maximum(
            jnp.max(first, axis=1, keepdims=True),
            jnp.max(jnp.where(low, tail, -jnp.inf), axis=1, keepdims=True),
        )
        second_max = jnp.maximum(
            jnp.max(second, axis=1, keepdims=True),
            jnp.max(jnp.where(low, -jnp.inf, tail), axis=1, keepdims=True),
        )
        exponent = jnp.concatenate(
            [
                jnp.exp(first - first_max).astype(BF16),
                jnp.exp(second - second_max).astype(BF16),
                jnp.exp(tail - jnp.where(low, first_max, second_max)).astype(BF16),
            ],
            axis=1,
        )
        weights_out[0, 0, rows] = exponent
        summed = dot(exponent, values)
        inverse = 1.0 / summed[:, PAIR:]
        inverse_out[0, 0, rows] = inverse
        context_out[0, pair, rows] = (summed[:, :PAIR] * inverse).astype(BF16)

    @pl.when(pair == pairs - 1)
    def _():
        context = jnp.concatenate([context_out[0, at] for at in range(pairs)], axis=1)
        residual = tokens[...].astype(F32) + (dot(context, w_proj[...]) + as_row(proj_bias))
        residual_out[...] = residual
        unit, _ = standardize(residual)
        normed = (unit * as_row(gain_two) + as_row(shift_two)).astype(BF16)
        normed_two_out[...] = normed


def front(tokens, w_qkv, q_bias, v_bias, w_proj, proj_bias, gain_one, shift_one, gain_two, shift_two):
    rows, width = tokens.shape
    images = rows // SEQ
    pairs = width // PAIR

    def per_image(columns):
        return pl.BlockSpec((SEQ, columns), lambda i, p: (i, 0))

    fixed = (w_qkv, q_bias, v_bias, w_proj, proj_bias, gain_one, shift_one, gain_two, shift_two)
    return pl.pallas_call(
        functools.partial(front_kernel, SEQ // 2),
        grid=(images, pairs),
        in_specs=[per_image(width)] + [whole(array) for array in fixed],
        out_specs=[
            per_image(width),
            pl.BlockSpec((1, 3 * pairs, SEQ, PAIR), lambda i, p: (i, 0, 0, 0)),
            pl.BlockSpec((1, 1, SEQ, 2 * SEQ), lambda i, p: (i, p, 0, 0)),
            pl.BlockSpec((1, 1, SEQ, PAIR), lambda i, p: (i, p, 0, 0)),
            pl.BlockSpec((1, pairs, SEQ, PAIR), lambda i, p: (i, 0, 0, 0)),
            per_image(width),
            per_image(width),
        ],
        out_shape=[
            shape((rows, width), BF16),
            shape((images, 3 * pairs, SEQ, PAIR), BF16),
            shape((images, pairs, SEQ, 2 * SEQ), BF16),
            shape((images, pairs, SEQ, PAIR), F32),
            shape((images, pairs, SEQ, PAIR), BF16),
            shape((rows, width), F32),
            shape((rows, width), BF16),
        ],
        scratch_shapes=[pltpu.VMEM((2 * SEQ, 2 * PAIR), BF16)],
        compiler_params=params(),
        cost_estimate=cost(30e9, 60e6),
        name="front",
    )(tokens, *fixed)


def columns_of(ids, slots, slot_count):
    return jnp.where(slots[...] >= 0, ids[...] * slot_count + slots[...], -1)


def gather_kernel(chunk, slot_count, ids, slots, rows, out):
    columns = columns_of(ids, slots, slot_count)
    at = pl.program_id(0) * chunk
    slot = at + lax.broadcasted_iota(jnp.int32, (chunk, columns.shape[1]), 0)
    hit = (columns[0:1, :] == slot) | (columns[1:2, :] == slot)
    out[...] = dot(jnp.where(hit, 1.0, 0.0).astype(BF16), rows[...]).astype(BF16)


def gather(ids, slots, rows, slot_count, chunk=288):
    count, width = rows.shape
    return pl.pallas_call(
        functools.partial(gather_kernel, chunk, slot_count),
        grid=(count // chunk,),
        in_specs=[whole(ids), whole(slots), whole(rows)],
        out_specs=pl.BlockSpec((chunk, width), lambda i: (i, 0)),
        out_shape=shape((count, width), BF16),
        compiler_params=params(),
        cost_estimate=cost(4e9, 8e6),
        name="gather",
    )(ids, slots, rows)


def raw_kernel(slot_count, ids, slots, cotangent, weight_out, out, columns_out):
    @pl.when(pl.program_id(0) == 0)
    def _():
        columns = columns_of(ids, slots, slot_count)
        pad = jnp.full((6, columns.shape[1]), -1, jnp.int32)
        columns_out[...] = jnp.concatenate([columns, pad], axis=0).T

    out[...] = dot_last(cotangent[...], weight_out[...]).astype(BF16)


def raw_active(ids, slots, cotangent, weight_out, slot_count, chunk=768):
    count, width = cotangent.shape
    hidden = weight_out.shape[0]
    return pl.pallas_call(
        functools.partial(raw_kernel, slot_count),
        grid=(hidden // chunk,),
        in_specs=[whole(ids), whole(slots), whole(cotangent), pl.BlockSpec((chunk, width), lambda i: (i, 0))],
        out_specs=[pl.BlockSpec((count, chunk), lambda i: (0, i)), pl.BlockSpec((count, 8), lambda i: (0, 0))],
        out_shape=[shape((count, hidden), BF16), shape((count, 8), jnp.int32)],
        compiler_params=params(),
        cost_estimate=cost(9e9, 14e6),
        name="raw_active",
    )(ids, slots, cotangent, weight_out)


def product_six(left, right):
    total = dot(left[0], right[0])
    for one, other in ((0, 1), (1, 0), (1, 1), (0, 2), (2, 0)):
        total += dot(left[one], right[other])
    return total


def expert_kernel(
    row_chunk,
    arrived,
    cotangent,
    weight_in,
    bias_in,
    raw,
    bias_out,
    w_router,
    active_out,
    hidden_out,
    weight_grad,
    bias_grad,
    out_bias_grad,
    gate_out,
    logits_grad,
    produced_grad,
    gate_total,
    router,
):
    step = pl.program_id(0)
    count = cotangent.shape[0]
    experts = w_router.shape[0]

    @pl.when(step == 0)
    def _():
        parts = thirds(w_router[...])
        logits = dot_last(arrived[...], parts[0]) + (
            dot_last(arrived[...], parts[1]) + dot_last(arrived[...], parts[2])
        )
        exponent = jnp.exp(logits - jnp.max(logits, axis=1, keepdims=True))
        probs = exponent / jnp.sum(exponent, axis=1, keepdims=True)
        router[...] = probs
        own = lax.broadcasted_iota(jnp.int32, (count, experts), 1) == lax.axis_index("exp")
        gate = jnp.sum(jnp.where(own, probs, 0.0), axis=1, keepdims=True)
        gate_out[...] = jnp.broadcast_to(gate, gate_out.shape)
        rows = cotangent[...].astype(F32)
        gated = (gate * rows).astype(BF16)
        produced_grad[...] = gated
        out_bias_grad[...] = column_sum(gated.astype(F32))
        along = jnp.sum(rows * bias_out[...], axis=1, keepdims=True)
        gate_total[...] = jnp.broadcast_to(along, gate_total.shape)

    sums = jnp.zeros(bias_grad.shape, F32)
    for at in range(0, count, row_chunk):
        rows = slice(at, at + row_chunk)
        hidden = dot(arrived[rows, :], weight_in[...]) + bias_in[...]
        cdf = 0.5 + 0.5 * lax.erf(hidden * (0.5**0.5))
        density = jnp.exp(hidden * hidden * -0.5) * (0.5 * 1.1283791670955126 * 0.5**0.5)
        active = (hidden * cdf).astype(BF16)
        incoming = raw[rows, :].astype(F32)
        gate_total[rows, :] += jnp.sum(active.astype(F32) * incoming, axis=1, keepdims=True)
        grad = (incoming * gate_out[rows, 0:1] * (cdf + hidden * density)).astype(BF16)
        active_out[rows, :] = active
        hidden_out[rows, :] = grad
        sums += column_sum(grad.astype(F32))
    bias_grad[...] = sums
    weight_grad[...] = dot_first(active_out[...], produced_grad[...]).astype(BF16)

    @pl.when(step == pl.num_programs(0) - 1)
    def _():
        own = lax.broadcasted_iota(jnp.int32, (count, experts), 1) == lax.axis_index("exp")
        scale = gate_total[:, 0:1] * gate_out[:, 0:1]
        logits_grad[...] = scale * (jnp.where(own, 1.0, 0.0) - router[...])


def expert(arrived, cotangent, weight_in, bias_in, raw, bias_out, w_router, chunk=512):
    count, width = cotangent.shape
    hidden = weight_in.shape[1]
    experts = w_router.shape[0]

    def column_block(rows):
        return pl.BlockSpec((rows, chunk), lambda i: (0, i))

    def fixed(rows, columns):
        return pl.BlockSpec((rows, columns), lambda i: (0, 0))

    return pl.pallas_call(
        functools.partial(expert_kernel, 288),
        grid=(hidden // chunk,),
        in_specs=[
            whole(arrived),
            whole(cotangent),
            column_block(width),
            column_block(1),
            column_block(count),
            whole(bias_out),
            whole(w_router),
        ],
        out_specs=[
            column_block(count),
            column_block(count),
            pl.BlockSpec((chunk, width), lambda i: (i, 0)),
            column_block(1),
            fixed(1, width),
            fixed(count, AUX),
            fixed(count, experts),
        ],
        out_shape=[
            shape((count, hidden), BF16),
            shape((count, hidden), BF16),
            shape((hidden, width), BF16),
            shape((1, hidden), F32),
            shape((1, width), F32),
            shape((count, AUX), F32),
            shape((count, experts), F32),
        ],
        scratch_shapes=[
            pltpu.VMEM((count, width), BF16),
            pltpu.VMEM((count, 128), F32),
            pltpu.VMEM((count, experts), F32),
        ],
        compiler_params=params(),
        cost_estimate=cost(24e9, 35e6),
        name="expert",
    )(arrived, cotangent, weight_in, bias_in, raw, bias_out, w_router)


def expert_back_kernel(grad_hidden, weight_in, logits_grad, w_router, arrived, out, router_grad):
    @pl.when(pl.program_id(0) == 0)
    def _():
        router_grad[...] = jnp.zeros_like(router_grad)

    left = thirds(logits_grad[...])
    total = dot_last(grad_hidden[...], weight_in[...]) + product_six(left, thirds(w_router[...]))
    out[...] = total.astype(BF16)
    for part in left:
        router_grad[...] += dot_first(part, arrived[...])


def expert_back(grad_hidden, weight_in, logits_grad, w_router, arrived, chunk=288):
    count, hidden = grad_hidden.shape
    experts, width = w_router.shape

    def rows(columns):
        return pl.BlockSpec((chunk, columns), lambda i: (i, 0))

    return pl.pallas_call(
        expert_back_kernel,
        grid=(count // chunk,),
        in_specs=[rows(hidden), whole(weight_in), rows(experts), whole(w_router), rows(width)],
        out_specs=[rows(width), pl.BlockSpec((experts, width), lambda i: (0, 0))],
        out_shape=[shape((count, width), BF16), shape((experts, width), F32)],
        compiler_params=params(),
        cost_estimate=cost(12e9, 15e6),
        name="expert_back",
    )(grad_hidden, weight_in, logits_grad, w_router, arrived)


def weight_in_kernel(arrived, grad_hidden, bias_grad, out_bias_grad, first, second, turned):
    width = turned.shape[0]
    half = width // 2

    @pl.when(pl.program_id(0) == 0)
    def _():
        turned[...] = arrived[...].T

    total = dot(turned[...], grad_hidden[...]).astype(BF16)
    first[0] = total[:half]
    second[0, :half] = total[half:]
    row = lax.broadcasted_iota(jnp.int32, (second.shape[1] - half, second.shape[2]), 0)
    second[0, half:] = jnp.where(row == 0, bias_grad[...], jnp.where(row == 1, out_bias_grad[0], 0.0)).astype(BF16)


def weight_in_grad(arrived, grad_hidden, bias_grad, out_bias_grad, width, reps):
    count, hidden = grad_hidden.shape
    part = hidden // reps
    return pl.pallas_call(
        weight_in_kernel,
        grid=(reps,),
        in_specs=[
            whole(arrived),
            pl.BlockSpec((count, part), lambda i: (0, i)),
            pl.BlockSpec((1, part), lambda i: (0, i)),
            pl.BlockSpec((1, 1, part), lambda i: (i, 0, 0)),
        ],
        out_specs=[
            pl.BlockSpec((1, width // 2, part), lambda i: (i, 0, 0)),
            pl.BlockSpec((1, width // 2 + 16, part), lambda i: (i, 0, 0)),
        ],
        out_shape=[shape((reps, width // 2, part), BF16), shape((reps, width // 2 + 16, part), BF16)],
        scratch_shapes=[pltpu.VMEM((width, count), BF16)],
        compiler_params=params(),
        cost_estimate=cost(10e9, 15e6),
        name="weight_in_grad",
    )(arrived, grad_hidden, bias_grad, out_bias_grad)


def produce_kernel(gate, active, weight_out, bias_out, out):
    out[...] = (gate[:, 0:1] * (dot(active[...], weight_out[...]) + bias_out[...])).astype(BF16)


def produce(gate, active, weight_out, bias_out, chunk=288):
    count, hidden = active.shape
    width = weight_out.shape[1]
    return pl.pallas_call(
        produce_kernel,
        grid=(count // chunk,),
        in_specs=[
            pl.BlockSpec((chunk, AUX), lambda i: (i, 0)),
            pl.BlockSpec((chunk, hidden), lambda i: (i, 0)),
            whole(weight_out),
            whole(bias_out),
        ],
        out_specs=pl.BlockSpec((chunk, width), lambda i: (i, 0)),
        out_shape=shape((count, width), BF16),
        compiler_params=params(),
        cost_estimate=cost(10e9, 15e6),
        name="produce",
    )(gate, active, weight_out, bias_out)


def token_hits(columns, slots):
    slot = lax.broadcasted_iota(jnp.int32, (columns.shape[0], slots), 1)
    hit = (columns[:, 0:1] == slot) | (columns[:, 1:2] == slot)
    return jnp.where(hit, 1.0, 0.0).astype(BF16)


def split_rows(value, kept, sent):
    half = value.shape[0] // 2
    first = (lax.axis_index("exp") & 1) == 0
    low, high = value[:half], value[half:]
    kept[...] = jnp.where(first, low, high)
    sent[...] = jnp.where(first, high, low)


def middle_kernel(
    sub,
    columns,
    source,
    residual,
    cotangent,
    context,
    w_proj,
    gain_two,
    grad_residual_out,
    grad_context_out,
    proj_kept,
    proj_sent,
    vectors,
    branch,
    proj_total,
):
    step = pl.program_id(0)
    chunk = residual.shape[0]
    pairs = context.shape[1]

    @pl.when(step == 0)
    def _():
        vectors[...] = jnp.zeros_like(vectors)
        proj_total[...] = jnp.zeros_like(proj_total)

    hits = token_hits(columns, source.shape[0])
    grad_residual_out[...] = dot(hits, source[...])
    gain = as_row(gain_two)
    for at in range(0, chunk, sub):
        rows = slice(at, at + sub)
        grad_normed = grad_residual_out[rows, :]
        unit, inverse = standardize(residual[rows, :])
        grad_residual = cotangent[rows, :].astype(F32) + standardize_back(grad_normed, gain, unit, inverse)
        grad_residual_out[rows, :] = grad_residual
        rounded = grad_residual.astype(BF16)
        branch[rows, :] = rounded
        vectors[0:1] += column_sum(grad_normed * unit)
        vectors[1:2] += column_sum(grad_normed)
        vectors[2:3] += column_sum(rounded.astype(F32))
    grad_context = dot_last(branch[...], w_proj[...]).astype(BF16)
    for pair in range(pairs):
        grad_context_out[0, pair] = grad_context[:, pair * PAIR : (pair + 1) * PAIR]
    joined = jnp.concatenate([context[0, pair] for pair in range(pairs)], axis=1)
    proj_total[...] += dot_first(joined, branch[...])

    @pl.when(step == pl.num_programs(0) - 1)
    def _():
        split_rows(proj_total[...].astype(BF16), proj_kept, proj_sent)


def middle(columns, source, residual, cotangent, context, w_proj, gain_two, chunk=288):
    rows, width = residual.shape
    images, pairs = context.shape[:2]
    parts = SEQ // chunk

    def rows_of(columns):
        return pl.BlockSpec((chunk, columns), lambda i: (i, 0))

    by_pair = pl.BlockSpec((1, pairs, chunk, PAIR), lambda i: (i // parts, 0, i % parts, 0))
    return pl.pallas_call(
        functools.partial(middle_kernel, 32),
        grid=(rows // chunk,),
        in_specs=[
            rows_of(8),
            whole(source),
            rows_of(width),
            rows_of(width),
            by_pair,
            whole(w_proj),
            whole(gain_two),
        ],
        out_specs=[
            rows_of(width),
            by_pair,
            pl.BlockSpec((width // 2, width), lambda i: (0, 0)),
            pl.BlockSpec((width // 2, width), lambda i: (0, 0)),
            pl.BlockSpec((8, width), lambda i: (0, 0)),
        ],
        out_shape=[
            shape((rows, width), F32),
            shape((images, pairs, SEQ, PAIR), BF16),
            shape((width // 2, width), BF16),
            shape((width // 2, width), BF16),
            shape((8, width), F32),
        ],
        scratch_shapes=[pltpu.VMEM((chunk, width), BF16), pltpu.VMEM((width, width), F32)],
        compiler_params=params(),
        cost_estimate=cost(14e9, 20e6),
        name="middle",
    )(columns, source, residual, cotangent, context, w_proj, gain_two)


def merge_heads(turned):
    first = jnp.concatenate([turned[:HEAD_DIM, :SPLIT], turned[:HEAD_DIM, 2 * SPLIT : SPLIT + SEQ]], axis=1)
    second = jnp.concatenate([turned[HEAD_DIM:, SPLIT : 2 * SPLIT], turned[HEAD_DIM:, SPLIT + SEQ :]], axis=1)
    return jnp.concatenate([first, second], axis=0).T


def attend_back_kernel(
    chunk,
    grad_context,
    queries,
    keys,
    values,
    weights,
    inverse,
    context,
    normed_one,
    grad_out,
    kept,
    sent,
    value_side,
    grad_scores,
):
    pair = pl.program_id(0)
    image = pl.program_id(1)

    @pl.when((pair == 0) & (image == 0))
    def _():
        is_first, lane = key_sides()
        taken = (is_first & (lane < 2)) | (jnp.logical_not(is_first) & (lane >= 2) & (lane < 4))
        value_side[:, PAIR:] = jnp.where(taken, -1.0, 0.0).astype(BF16)

    key_side = split_heads(keys[0, 0])
    value_side[:, :PAIR] = split_heads(values[0, 0])
    lane = lax.broadcasted_iota(jnp.int32, (chunk, PAIR), 1)
    low = lane < HEAD_DIM
    scaled = []
    for at in range(0, SEQ, chunk):
        rows = slice(at, at + chunk)
        grads = (grad_context[0, 0, rows].astype(F32) * inverse[0, 0, rows]).astype(BF16)
        scaled.append(grads)
        product = grads.astype(F32) * context[0, 0, rows].astype(F32)
        first = jnp.sum(jnp.where(low, product, 0.0), axis=1, keepdims=True)
        second = jnp.sum(jnp.where(low, 0.0, product), axis=1, keepdims=True)
        offset = jnp.where(lane < 2, first, second)
        high = offset.astype(BF16).astype(F32)
        extra = jnp.where(
            (lane == 0) | (lane == 2), high, jnp.where((lane == 1) | (lane == 3), offset - high, 0.0)
        ).astype(BF16)
        grad_weights = dot_last(jnp.concatenate([grads, extra], axis=1), value_side[...])
        part = grad_weights.astype(BF16) * weights[0, 0, rows]
        grad_scores[rows] = part
        place = pl.ds(pl.multiple_of(image * SEQ + at, 32), chunk)
        grad_out[0, pair, place] = (dot(part, key_side) * HEAD_DIM**-0.5).astype(BF16)
    grads = jnp.concatenate(scaled, axis=0)
    place = pl.ds(pl.multiple_of(image * SEQ, 64), SEQ)
    grad_out[1, pair, place] = merge_heads(dot_first(queries[0, 0], grad_scores[...])).astype(BF16)
    grad_out[2, pair, place] = merge_heads(dot_first(grads, weights[0, 0])).astype(BF16)

    @pl.when((pair == pl.num_programs(0) - 1) & (image == pl.num_programs(1) - 1))
    def _():
        for kind in range(3):
            joined = jnp.concatenate([grad_out[kind, at] for at in range(grad_out.shape[1])], axis=1)
            span = joined.shape[1]
            columns = slice(kind * span, (kind + 1) * span)
            total = dot_first(normed_one[...], joined).astype(BF16)
            split_rows(total, kept.at[:, columns], sent.at[:, columns])


def attend_back(grad_context, qkv, weights, inverse, context, normed_one, first, count):
    images, pairs = context.shape[:2]
    rows, width = normed_one.shape

    def block(offset):
        return pl.BlockSpec((1, 1, SEQ, PAIR), lambda p, i: (i, offset + p, 0, 0))

    return pl.pallas_call(
        functools.partial(attend_back_kernel, SEQ),
        grid=(count, images),
        in_specs=[
            block(first),
            block(first),
            block(pairs + first),
            block(2 * pairs + first),
            pl.BlockSpec((1, 1, SEQ, 2 * SEQ), lambda p, i: (i, first + p, 0, 0)),
            block(first),
            block(first),
            whole(normed_one),
        ],
        out_specs=[
            pl.BlockSpec((3, count, rows, PAIR), lambda p, i: (0, 0, 0, 0)),
            pl.BlockSpec((width // 2, 3 * count * PAIR), lambda p, i: (0, 0)),
            pl.BlockSpec((width // 2, 3 * count * PAIR), lambda p, i: (0, 0)),
        ],
        out_shape=[shape((3, count, rows, PAIR), BF16)] + [shape((width // 2, 3 * count * PAIR), BF16)] * 2,
        scratch_shapes=[pltpu.VMEM((2 * SEQ, 2 * PAIR), BF16), pltpu.VMEM((SEQ, 2 * SEQ), BF16)],
        compiler_params=params(),
        cost_estimate=cost(17e9 * (100 if first else 1), 20e6 * (100 if first else 1)),
        name="attend_back",
    )(grad_context, qkv, qkv, qkv, weights, inverse, context, normed_one)


def last_kernel(groups, sub, tokens, w_qkv, grad_residual, gain_one, *rest):
    grads = rest[:groups]
    out, vectors = rest[groups:]
    width = tokens.shape[1]

    @pl.when(pl.program_id(0) == 0)
    def _():
        vectors[...] = jnp.zeros_like(vectors)

    total = jnp.zeros(tokens.shape, F32)
    for kind in range(3):
        joined = jnp.concatenate(
            [grad[kind, at] for grad in grads for at in range(grad.shape[1])], axis=1
        )
        total += dot_last(joined, w_qkv[:, kind * width : (kind + 1) * width])
        if kind == 0:
            vectors[2:3] += column_sum(joined.astype(F32))
        if kind == 2:
            vectors[3:4] += column_sum(joined.astype(F32))
    out[...] = total
    gain = as_row(gain_one)
    for at in range(0, tokens.shape[0], sub):
        rows = slice(at, at + sub)
        grad_normed = out[rows, :]
        unit, inverse = standardize(tokens[rows, :].astype(F32))
        out[rows, :] = grad_residual[rows, :] + standardize_back(grad_normed, gain, unit, inverse)
        vectors[0:1] += column_sum(grad_normed * unit)
        vectors[1:2] += column_sum(grad_normed)


def last(tokens, grads, w_qkv, grad_residual, gain_one, chunk=288):
    rows, width = tokens.shape
    block = pl.BlockSpec((chunk, width), lambda i: (i, 0))
    return pl.pallas_call(
        functools.partial(last_kernel, len(grads), 32),
        grid=(rows // chunk,),
        in_specs=[block, whole(w_qkv), block, whole(gain_one)]
        + [pl.BlockSpec((3, grad.shape[1], chunk, PAIR), lambda i: (0, 0, i, 0)) for grad in grads],
        out_specs=[block, pl.BlockSpec((8, width), lambda i: (0, 0))],
        out_shape=[shape((rows, width), F32), shape((8, width), F32)],
        compiler_params=params(),
        cost_estimate=cost(10e9, 15e6),
        name="last",
    )(tokens, w_qkv, grad_residual, gain_one, *grads)


def fold_kernel(count, *refs):
    inputs, outs = refs[: 2 * count], refs[2 * count :]
    at = lax.axis_index("exp") >> 1
    rows = outs[0].shape[0]
    for other, out in enumerate(outs):
        here = pl.ds(pl.multiple_of((at ^ other) * rows, rows), rows)
        column = 0
        for kept, received in zip(inputs[:count], inputs[count:]):
            span = slice(column, column + kept.shape[1])
            out[:, span] = (kept[here, :].astype(F32) + received[here, :].astype(F32)).astype(BF16)
            column = span.stop


def fold(kept, received, chips):
    rows = kept[0].shape[0] // chips
    width = sum(part.shape[1] for part in kept)
    return pl.pallas_call(
        functools.partial(fold_kernel, len(kept)),
        out_shape=[shape((rows, width), BF16)] * chips,
        compiler_params=params(),
        cost_estimate=cost(1e9, 10e6),
        name="fold",
    )(*kept, *received)


def finish_kernel(left, where, *refs):
    inputs, (proj_out, out) = refs[:-2], refs[-2:]
    width = proj_out.shape[1]
    right = width - left
    for step, part in enumerate(inputs):

        @pl.when(pl.program_id(0) == step)
        def _():
            proj_out[...] = part[:, :width].astype(F32)
            for kind in range(3):
                to = kind * width
                at = width + kind * left
                out[:, to : to + left] = part[:, at : at + left].astype(F32)
                at = width + 3 * left + kind * right
                out[:, to + left : to + width] = part[:, at : at + right].astype(F32)


def finish(parts, where, left):
    steps = len(parts)
    rows = parts[0].shape[0]
    width = parts[0].shape[1] // 4

    def landing(columns):
        return pl.BlockSpec((rows, columns), lambda i, at: (at[i], 0))

    return pl.pallas_call(
        functools.partial(finish_kernel, left),
        grid_spec=pltpu.PrefetchScalarGridSpec(
            num_scalar_prefetch=1,
            grid=(steps,),
            in_specs=[pl.BlockSpec(part.shape, lambda i, at: (0, 0)) for part in parts],
            out_specs=[landing(width), landing(3 * width)],
        ),
        out_shape=[shape((rows * steps, width), F32), shape((rows * steps, 3 * width), F32)],
        compiler_params=params(),
        cost_estimate=cost(1e9, 10e6),
        name="finish",
    )(where, *parts)


def combine_kernel(columns, source, residual, out):
    hits = token_hits(columns, source.shape[0])
    out[...] = (residual[...] + dot(hits, source[...])).astype(BF16)


def combine(columns, source, residual, chunk=288):
    rows, width = residual.shape
    return pl.pallas_call(
        combine_kernel,
        grid=(rows // chunk,),
        in_specs=[
            pl.BlockSpec((chunk, 8), lambda i: (i, 0)),
            whole(source),
            pl.BlockSpec((chunk, width), lambda i: (i, 0)),
        ],
        out_specs=pl.BlockSpec((chunk, width), lambda i: (i, 0)),
        out_shape=shape((rows, width), BF16),
        compiler_params=params(),
        cost_estimate=cost(6e9, 10e6),
        name="combine",
    )(columns, source, residual)


def exchange(rows, experts):
    blocks = rows.reshape(experts, rows.shape[0] // experts, rows.shape[1])
    return lax.all_to_all(blocks, "exp", split_axis=0, concat_axis=0, tiled=True).reshape(rows.shape)


def share(block, name, size):
    copies = jnp.broadcast_to(block[None], (size,) + block.shape)
    return lax.all_to_all(copies, name, split_axis=0, concat_axis=0, tiled=True)


def sum_blocks(blocks, kind):
    return jnp.sum(blocks.astype(F32), axis=0).astype(kind)


def scatter_reps(blocks):
    rows = blocks.reshape((-1,) + blocks.shape[2:])
    return lax.psum_scatter(rows, "rep", scatter_dimension=0, tiled=True)


def swap(block, name, bits, size):
    return lax.ppermute(block, name, [(at, at ^ bits) for at in range(size)])


def chip_scatter(kept, sent, sizes):
    size = sizes["exp"]
    chips = size // 2
    received = [swap(part, "exp", 1, size) for part in sent]
    parts = fold(kept, received, chips)
    return parts


def plane_sum(parts, sizes):
    size = sizes["exp"]
    chips = size // 2
    received = [swap(parts[other], "exp", 2 * other, size) for other in range(1, chips)]
    total = parts[0].astype(F32)
    for part in received:
        total += part.astype(F32)
    return total.astype(BF16)


def rep_sum(block, sizes):
    reps = sizes["rep"]
    blocks = block.reshape((reps, -1) + block.shape[1:])
    at = lax.convert_element_type(lax.axis_index("rep"), jnp.uint32)

    def pick(other):
        return lax.dynamic_index_in_dim(blocks, at ^ jnp.uint32(other), 0, keepdims=False)

    received = [swap(pick(other), "rep", other, reps) for other in range(1, reps)]
    total = pick(0).astype(F32)
    for part in received:
        total += part.astype(F32)
    return total.astype(BF16)


def rep_gather(block, sizes):
    reps = sizes["rep"]
    at = lax.axis_index("rep")
    parts = [block] + [swap(block, "rep", other, reps) for other in range(1, reps)]
    rows = []
    for slot in range(reps):
        chosen = parts[0]
        for other in range(1, reps):
            chosen = jnp.where((at ^ other) == slot, parts[other], chosen)
        rows.append(chosen)
    return jnp.concatenate(rows, axis=0)


def plane_gather(block, sizes):
    size = sizes["exp"]
    mine = [block] + [swap(block, "exp", 2 * other, size) for other in range(1, size // 2)]
    return mine + [swap(part, "exp", 1, size) for part in mine]


def join_halves(kept, sent):
    first = (lax.axis_index("exp") & 1) == 0
    return jnp.where(first, jnp.concatenate([kept, sent]), jnp.concatenate([sent, kept]))


def small_sums(vectors_two, vectors_one, router_grad):
    blank = jnp.zeros_like(vectors_one[:1])
    return jnp.concatenate([vectors_two[:3], vectors_one[:4], blank, router_grad], axis=0)


def tie(value, *after):
    return lax.optimization_barrier((value,) + after)[0]


def on_device(
    sizes,
    tokens,
    cotangent,
    expert_ids,
    expert_slots,
    w_qkv,
    q_bias,
    v_bias,
    w_proj,
    proj_bias,
    gain_one,
    shift_one,
    gain_two,
    shift_two,
    w_router,
    expert_in,
    expert_in_bias,
    expert_out,
    expert_out_bias,
):
    row_count, width = tokens.shape
    experts = w_router.shape[1]
    slot_count = row_count // experts
    reps = sizes["rep"]
    ids = expert_ids.T
    slots = expert_slots.T
    router_turned = w_router.T
    weight_in = expert_in[0]
    weight_out = expert_out[0]
    bias_in = expert_in_bias.astype(F32)
    bias_out = expert_out_bias.astype(F32)

    cot_arrived = exchange(gather(ids, slots, cotangent, slot_count), experts)
    normed_one, qkv, weights, inverse, context, residual, normed_two = front(
        tokens, w_qkv, q_bias.astype(F32), v_bias.astype(F32), w_proj, proj_bias.astype(F32), gain_one, shift_one, gain_two, shift_two
    )
    arrived = exchange(gather(ids, slots, normed_two, slot_count), experts)
    raw, columns = raw_active(ids, slots, cot_arrived, weight_out, slot_count)
    active, grad_hidden, out_grad, in_bias_grad, out_bias_grad, gate, logits_grad = expert(
        arrived, cot_arrived, weight_in, bias_in, raw, bias_out, router_turned
    )
    grad_eout = lax.psum_scatter(out_grad, "rep", scatter_dimension=0, tiled=True)
    back, router_grad = expert_back(grad_hidden, weight_in, logits_grad, router_turned, arrived)
    source = exchange(back, experts)
    part = weight_in.shape[1] // reps
    out_part = width // reps
    tail = jnp.pad(out_bias_grad.reshape(reps, 1, out_part), ((0, 0), (0, 0), (0, part - out_part)))
    in_first, in_second = weight_in_grad(arrived, grad_hidden, in_bias_grad, tail, width, reps)
    made = produce(gate, active, weight_out, bias_out)
    source, made, in_first, in_second = lax.optimization_barrier((source, made, in_first, in_second))
    in_first = scatter_reps(in_first)
    returned = exchange(made, experts)
    grad_residual, grad_context, proj_kept, proj_sent, vectors_two = middle(
        columns, source, residual, cotangent, context, w_proj, gain_two
    )
    pairs = width // PAIR
    most = pairs - pairs // 3
    saved = (qkv, weights, inverse, context, normed_one)
    grads_a, kept_a, sent_a = attend_back(grad_context, *saved, 0, most)
    chips = sizes["exp"] // 2
    if (width // sizes["exp"]) % 16 == 0:
        sent_a, proj_sent, returned = lax.optimization_barrier((sent_a, proj_sent, returned))
        parts_a = chip_scatter((proj_kept, kept_a), (proj_sent, sent_a), sizes)
        sum_a = plane_sum(parts_a, sizes)
        grads_b, kept_b, sent_b = attend_back(
            tie(grad_context, grads_a, parts_a[0], grad_eout), *saved, most, pairs - most
        )
        parts_b = chip_scatter((kept_b,), (sent_b,), sizes)
        sum_b = plane_sum(parts_b, sizes)
        mixed = combine(columns, tie(returned, parts_b[0]), residual)
        sum_a, sum_b, mixed, in_first = lax.optimization_barrier((sum_a, sum_b, mixed, in_first))
        block = jnp.concatenate([sum_a, sum_b], axis=1)
        grad_tokens, vectors_one = last(
            tokens, (grads_a, grads_b), w_qkv, tie(grad_residual, block), gain_one
        )
        block = rep_sum(block, sizes)
        block, vectors_one, grad_eout = lax.optimization_barrier((block, vectors_one, grad_eout))
        small = small_sums(vectors_two, vectors_one, router_grad)
        small = sum_blocks(share(small, "exp", sizes["exp"]), F32)
        block = rep_gather(block, sizes)
        block, in_second = lax.optimization_barrier((block, in_second))
        in_second = scatter_reps(in_second)
        small = sum_blocks(share(small, "rep", reps), F32)
        parts = plane_gather(block, sizes)
        here = lax.axis_index("exp")
        order = jnp.arange(chips, dtype=jnp.int32) ^ (here >> 1)
        core = here & 1
        where = jnp.concatenate([core * chips + order, (1 - core) * chips + order]).astype(jnp.int32)
        grad_w_proj, grad_w_qkv = finish(parts, where, most * PAIR)
    else:
        in_second = scatter_reps(in_second)
        grads_b, kept_b, sent_b = attend_back(grad_context, *saved, most, pairs - most)
        mixed = combine(columns, returned, residual)
        grad_tokens, vectors_one = last(tokens, (grads_a, grads_b), w_qkv, grad_residual, gain_one)
        block = join_halves(
            jnp.concatenate([proj_kept, kept_a, kept_b], axis=1),
            jnp.concatenate([proj_sent, sent_a, sent_b], axis=1),
        )
        small = lax.psum(small_sums(vectors_two, vectors_one, router_grad), ("rep", "exp"))
        block = lax.psum(block, ("rep", "exp"))
        where = jnp.zeros((1,), jnp.int32)
        grad_w_proj, grad_w_qkv = finish((block,), where, most * PAIR)
    return (
        mixed,
        grad_tokens,
        grad_w_qkv,
        small[5],
        small[6],
        grad_w_proj,
        small[2],
        small[3],
        small[4],
        small[0],
        small[1],
        small[8 : 8 + experts].T,
        jnp.concatenate([in_first, in_second[: width // 2]], axis=0)[None].astype(F32),
        in_second[width // 2 : width // 2 + 1].astype(F32),
        grad_eout[None].astype(F32),
        in_second[width // 2 + 1 : width // 2 + 2, :out_part].astype(F32),
    )


def solution(mesh):
    rows = P(("rep", "exp"), None)
    placed = (rows,) * 4 + (P(),) * 10 + (
        P("exp", None, None),
        P("exp", None),
        P("exp", None, None),
        P("exp", None),
    )
    return jax.shard_map(
        functools.partial(on_device, dict(mesh.shape)),
        mesh=mesh,
        in_specs=placed,
        out_specs=(rows, rows)
        + (P(),) * 10
        + (P("exp", None, "rep"), P("exp", "rep"), P("exp", "rep", None), P("exp", "rep")),
        check_vma=False,
    )
```

time: 427 us -> 352 us (0.82)
  the two profiles are of different devices: /device:TPU:27 before, /device:TPU:0 now
where the time goes in v2:
time: 352 us; the launch traced here: 351 us
  Pallas kernels  195 us (55%)
  waiting for transfers between devices  73.9 us (21%)
  starting transfers between devices  47.4 us (13%)
  between operations  14.1 us (4%)
  local copies, waits for them, and re-layouts  10.4 us (3%)
  other arithmetic  9.87 us (3%)
    pallas_call x2, Pallas kernels, attend_back(): pl.pallas_call(functools.partial(attend_back_kernel, SEQ), grid=(count, i...  35.4 us
    all_to_all x2, waiting for transfers between devices, share(): return lax.all_to_all(copies, name, split_axis=0, concat_axis=0, tiled=True)  33.7 us
    pallas_call x1, Pallas kernels, front(): pl.pallas_call(functools.partial(front_kernel, SEQ // 2), grid=(images, p...  31.8 us
    ppermute x22, waiting for transfers between devices, swap(): return lax.ppermute(block, name, [(at, at ^ bits) for at in range(size)])  26.7 us
    pallas_call x1, Pallas kernels, expert(): pl.pallas_call(functools.partial(expert_kernel, 288), grid=(hidden // chu...  25.9 us
    ppermute x22, starting transfers between devices, swap(): return lax.ppermute(block, name, [(at, at ^ bits) for at in range(size)])  22.9 us
    all_to_all x4, starting transfers between devices, exchange(): lax.all_to_all(blocks, 'exp', split_axis=0, concat_axis=0, tiled=True)  16.8 us
    pallas_call x1, Pallas kernels, middle(): pl.pallas_call(functools.partial(middle_kernel, 32), grid=(rows // chunk,...  14.8 us
  transfers between devices with their start and end apart: 31, of which 11 were waited for; matrix products, arithmetic and copies ran while one was open for 3% of the time, Pallas kernels for 47%

profile of v2, /device:TPU:0, one launch (start us, length us, event | category | flops | bytes accessed | tf_op | source)
XLA Modules:
  0.0 350.8 jit_solution(6848535778843338042)
XLA Ops:
  7.2 5.5 %gather.2 = bf16[1152,768]{1,0:T(8,128)(2,1)} custom-call(s32[2,1152]{1,0:T(2,128)} %bitcast.56, s32[2,1152]{1,0:T(2,128)} %bitcast.59, bf16[1152,768]{1,0:T(8,128)(2,1)} %cotangent.1), custom_call_target="tpu_custom_call" | custom-call | flops 40000000 | bytes 80000 | tf_op jit(solution)/shard_map/gather/pallas_call | solution.py:237
  12.7 5.3 %all-to-all-start = ((bf16[8,144,768]{2,1,0:T(8,128)(2,1)}), bf16[8,144,768]{2,1,0:T(8,128)(2,1)S(1)}, u32[]{:S(2)}, u32[]{:S(2)}) async-start(bf16[8,144,768]{2,1,0:T(8,128)(2,1)} %bitcast.44), calls=%async_computation | async-start | bytes 3538944 | tf_op jit(solution)/shard_map/all_to_all | solution.py:837
  19.8 31.8 %front.1 = (bf16[1152,768]{1,0:T(8,128)(2,1)}, bf16[2,18,576,128]{3,2,1,0:T(8,128)(2,1)}, bf16[2,6,576,1152]{3,2,1,0:T(8,128)(2,1)}, f32[2,6,576,128]{3,2,1,0:T(...) custom-call(bf16[1152,768]{1,0:T(8,128)(2,1)} %tokens.3, ...), custom_call_target="tpu_custom_call" | custom-call | flops 300000000 | bytes 600000 | tf_op jit(solution)/shard_map/front/pallas_call | solution.py:194
  51.6 5.5 %gather.3 = bf16[1152,768]{1,0:T(8,128)(2,1)} custom-call(s32[2,1152]{1,0:T(2,128)} %bitcast.57, s32[2,1152]{1,0:T(2,128)} %bitcast.60, bf16[1152,768]{1,0:T(8,128)(2,1)} %get-tuple-element.79.rows), custom_call_target="tpu_custom_call" | custom-call | flops 40000000 | bytes 80000 | tf_op jit(solution)/shard_map/gather/pallas_call | solution.py:237
  58.4 4.2 %all-to-all-start.1 = ((bf16[8,144,768]{2,1,0:T(8,128)(2,1)}), bf16[8,144,768]{2,1,0:T(8,128)(2,1)S(1)}, u32[]{:S(2)}, u32[]{:S(2)}) async-start(bf16[8,144,768]{2,1,0:T(8,128)(2,1)} %bitcast.45), calls=%async_computation.1 | async-start | bytes 3538944 | tf_op jit(solution)/shard_map/all_to_all | solution.py:837
  64.0 10.1 %raw_active.1 = (bf16[1152,3072]{1,0:T(8,128)(2,1)}, s32[1152,8]{1,0:T(8,128)}) custom-call(s32[2,1152]{1,0:T(2,128)} %bitcast.58, s32[2,1152]{1,0:T(2,128)} %bitcast.61, bf16[1152,768]{1,0:T(8,128)(2,1)} %bitcast.41, bf16[3072,768]{1,0:T(8,128)(2,1)} %bitcast.39), custom_call_target="tpu_custom_call" | custom-call | flops 90000000 | bytes 140000 | tf_op jit(solution)/shard_map/raw_active/pallas_call | solution.py:262
  74.1 11.6 %all-to-all-done.1 = bf16[8,144,768]{2,1,0:T(8,128)(2,1)S(1)} async-done(((bf16[8,144,768]{2,1,0:T(8,128)(2,1)}), bf16[8,144,768]{2,1,0:T(8,128)(2,1)S(1)}, u32[]{:S(2)}, u32[]{:S(2)}) %all-to-all-start.1) | async-done | bytes 1769504 | tf_op jit(solution)/shard_map/all_to_all | solution.py:837
  86.9 25.9 %expert.1 = (bf16[1152,3072]{1,0:T(8,128)(2,1)}, bf16[1152,3072]{1,0:T(8,128)(2,1)}, bf16[3072,768]{1,0:T(8,128)(2,1)}, f32[1,3072]{1,0:T(1,128)}, f32[1,768]{1,...) custom-call(bf16[1152,768]{1,0:T(8,128)(2,1)} %bitcast.34, bf16[1152,768]{1,0:T(8,128)(2,1)} %bitcast.42, ...), custom_call_target="tpu_custom_call" | custom-call | flops 240000000 | bytes 350000 | tf_op jit(solution)/shard_map/expert/pallas_call | solution.py:358
  112.8 13.5 %expert_back.1 = (bf16[1152,768]{1,0:T(8,128)(2,1)}, f32[8,768]{1,0:T(8,128)}) custom-call(bf16[1152,3072]{1,0:T(8,128)(2,1)} %get-tuple-element.81.grad_hidden, bf16[768,3072]{1,0:T(8,128)(2,1)} %bitcast.38, f32[1152,8]{1,0:T(8,128)} %get-tuple-element.82.logits_grad, f32[8,768]{1,0:T(8,128)} %bitcast.55, bf16[1152,768]{1,0:T(8,128)(2,1)} %bitcast.35), custom_call_target="tpu_custom_call" | custom-call | flops 120000000 | bytes 150000 | tf_op jit(solution)/shard_map/expert_back/pallas_call | solution.py:418
  126.3 3.7 %all-to-all-start.2 = ((bf16[8,144,768]{2,1,0:T(8,128)(2,1)}), bf16[8,144,768]{2,1,0:T(8,128)(2,1)S(1)}, u32[]{:S(2)}, u32[]{:S(2)}) async-start(bf16[8,144,768]{2,1,0:T(8,128)(2,1)} %bitcast.52), calls=%async_computation.2 | async-start | bytes 3538944 | tf_op jit(solution)/shard_map/all_to_all | solution.py:837
  130.7 10.1 %produce.1 = bf16[1152,768]{1,0:T(8,128)(2,1)} custom-call(f32[1152,128]{1,0:T(8,128)} %get-tuple-element.84.gate, bf16[1152,3072]{1,0:T(8,128)(2,1)} %get-tuple-element.85.active, bf16[3072,768]{1,0:T(8,128)(2,1)} %bitcast.40, f32[1,768]{1,0:T(1,128)} %convert_element_type.95.bias_out), custom_call_target="tpu_custom_call" | custom-call | flops 100000000 | bytes 150000 | tf_op jit(solution)/shard_map/produce/pallas_call | solution.py:476
  140.9 11.1 %weight_in_grad.1 = (bf16[4,384,768]{2,1,0:T(8,128)(2,1)}, bf16[4,400,768]{2,1,0:T(8,128)(2,1)}) custom-call(bf16[1152,768]{1,0:T(8,128)(2,1)} %bitcast.36, bf16[1152,3072]{1,0:T(8,128)(2,1)} %get-tuple-element.81.grad_hidden, f32[1,3072]{1,0:T(1,128)} %get-tuple-element.86.bias_grad, f32[4,1,768]{2,1,0:T(1,128)} %pad.4.out_bias_grad), custom_call_target="tpu_custom_call" | custom-call | flops 100000000 | bytes 150000 | tf_op jit(solution)/shard_map/weight_in_grad/pallas_call | solution.py:448
  154.3 3.6 %all-to-all-start.3 = ((bf16[8,144,768]{2,1,0:T(8,128)(2,1)}), bf16[8,144,768]{2,1,0:T(8,128)(2,1)S(1)}, u32[]{:S(2)}, u32[]{:S(2)}) async-start(bf16[8,144,768]{2,1,0:T(8,128)(2,1)} %bitcast.47), calls=%async_computation.3 | async-start | bytes 3538944 | tf_op jit(solution)/shard_map/all_to_all | solution.py:837
  158.9 14.8 %middle.1 = (f32[1152,768]{1,0:T(8,128)}, bf16[2,6,576,128]{3,2,1,0:T(8,128)(2,1)}, bf16[384,768]{1,0:T(8,128)(2,1)}, bf16[384,768]{1,0:T(8,128)(2,1)}, f32[8,768]{1,0:T(8,128)}) custom-call(s32[1152,8]{1,0:T(8,128)} %get-tuple-element.78.columns, bf16[1152,768]{1,0:T(8,128)(2,1)} %bitcast.43, f32[1152,768]{1,0:T(8,128)} %get-tuple-element.91.residual, ...), custom_call_target="tpu_custom_call" | custom-call | flops 140000000 | bytes 200000 | tf_op jit(solution)/shard_map/middle/pallas_call | solution.py:567
  173.7 22.3 %attend_back.2 = (bf16[3,4,1152,128]{3,2,1,0:T(8,128)(2,1)}, bf16[384,1536]{1,0:T(8,128)(2,1)}, bf16[384,1536]{1,0:T(8,128)(2,1)}) custom-call(bf16[2,6,576,128]{3,2,1,0:T(8,128)(2,1)} %get-tuple-element.111.grad_context, bf16[2,18,576,128]{3,2,1,0:T(8,128)(2,1)} %get-tuple-element.95.queries.keys.values, ...), custom_call_target="tpu_custom_call" | custom-call | flops 170000000 | bytes 200000 | tf_op jit(solution)/shard_map/attend_back/pallas_call | solution.py:675
  196.6 3.2 collective-permute-done.refs_2_
  201.0 3.6 %fold.2 = (bf16[96,2304]{1,0:T(8,128)(2,1)}, bf16[96,2304]{1,0:T(8,128)(2,1)}, bf16[96,2304]{1,0:T(8,128)(2,1)}, bf16[96,2304]{1,0:T(8,128)(2,1)}) custom-call(bf16[384,768]{1,0:T(8,128)(2,1)} %get-tuple-element.93.refs_0_, bf16[384,1536]{1,0:T(8,128)(2,1)} %get-tuple-element.99.refs_1_, bf16[384,768]{1,0:T(8,128)(2,1)} %copy-done.10, ...), custom_call_target="tpu_custom_call" | custom-call | flops 10000000 | bytes 100000 | tf_op jit(solution)/shard_map/fold/pallas_call | solution.py:763
  204.6 13.1 %attend_back.3 = (bf16[3,2,1152,128]{3,2,1,0:T(8,128)(2,1)}, bf16[384,768]{1,0:T(8,128)(2,1)}, bf16[384,768]{1,0:T(8,128)(2,1)}) custom-call(bf16[2,6,576,128]{3,2,1,0:T(8,128)(2,1)} %get-tuple-element.111.grad_context, bf16[2,18,576,128]{3,2,1,0:T(8,128)(2,1)} %get-tuple-element.95.queries.keys.values, ...), custom_call_target="tpu_custom_call" | custom-call | flops 16999999488 | bytes 20000000 | tf_op jit(solution)/shard_map/attend_back/pallas_call | solution.py:675
  218.2 2.6 collective-permute-start.4
  227.7 4.6 %collective-permute-done.4 = bf16[96,2304]{1,0:T(8,128)(2,1)S(1)} collective-permute-done((bf16[96,2304]{1,0:T(8,128)(2,1)}, bf16[96,2304]{1,0:T(8,128)(2,1)S(1)}, u32[]{:S(2)}, u32[]{:S(2)}) %collective-permute-start.4) | collective-permute-done | bytes 442400 | tf_op jit(solution)/shard_map/ppermute | solution.py:855
  233.9 7.9 %collective-permute-done.3 = bf16[96,2304]{1,0:T(8,128)(2,1)S(1)} collective-permute-done((bf16[96,2304]{1,0:T(8,128)(2,1)S(1)}, bf16[96,2304]{1,0:T(8,128)(2,1)S(1)}, u32[]{:S(2)}, u32[]{:S(2)}) %collective-permute-start.3) | collective-permute-done | bytes 442400 | tf_op jit(solution)/shard_map/ppermute | solution.py:855
  242.2 7.0 %combine.1 = bf16[1152,768]{1,0:T(8,128)(2,1)} custom-call(s32[1152,8]{1,0:T(8,128)} %get-tuple-element.78.columns, bf16[1152,768]{1,0:T(8,128)(2,1)} %bitcast.46, f32[1152,768]{1,0:T(8,128)} %get-tuple-element.91.residual), custom_call_target="tpu_custom_call" | custom-call | flops 60000000 | bytes 100000 | tf_op jit(solution)/shard_map/combine/pallas_call | solution.py:819
  249.4 4.0 %collective-permute-start.11 = (bf16[24,3072]{1,0:T(8,128)(2,1)S(1)}, bf16[24,3072]{1,0:T(8,128)(2,1)S(1)}, u32[]{:S(2)}, u32[]{:S(2)}) collective-permute-start(bf16[24,3072]{1,0:T(8,128)(2,1)S(1)} %get-tuple-element.152), channel_id=1, source_target_pairs={{0,24},{8,16},{16,8},{24,0},{1,25},{9,17},{17,9},{25,1},{2,26},{10... | collective-permute-start | bytes 442376 | tf_op jit(solution)/shard_map/ppermute | solution.py:855
  254.0 10.8 %last.1 = (f32[1152,768]{1,0:T(8,128)}, f32[8,768]{1,0:T(8,128)}) custom-call(bf16[1152,768]{1,0:T(8,128)(2,1)} %tokens.3, bf16[768,2304]{1,0:T(8,128)(2,1)} %w_qkv.3, f32[1152,768]{1,0:T(8,128)} %get-tuple-element.125.grad_residual, f32[768]{0:T(1024)} %gain_one.3, bf16[3,4,1152,128]{3,2,1,0:T(8,128)(2,1)} %get-tuple-element.109.rest_0_, ...), custom_call_target="tpu_custom_call" | custom-call | flops 100000000 | bytes 150000 | tf_op jit(solution)/shard_map/last/pallas_call | solution.py:734
  265.5 3.2 collective-permute-start.12
  270.0 4.2 %collective-permute-done.12 = bf16[24,3072]{1,0:T(8,128)(2,1)S(1)} collective-permute-done((bf16[24,3072]{1,0:T(8,128)(2,1)S(1)}, bf16[24,3072]{1,0:T(8,128)(2,1)S(1)}, u32[]{:S(2)}, u32[]{:S(2)}) %collective-permute-start.12) | collective-permute-done | bytes 147488 | tf_op jit(solution)/shard_map/ppermute | solution.py:855
  274.2 5.9 %collective-permute-done.13 = bf16[24,3072]{1,0:T(8,128)(2,1)S(1)} collective-permute-done((bf16[24,3072]{1,0:T(8,128)(2,1)S(1)}, bf16[24,3072]{1,0:T(8,128)(2,1)S(1)}, u32[]{:S(2)}, u32[]{:S(2)}) %collective-permute-start.13) | collective-permute-done | bytes 147488 | tf_op jit(solution)/shard_map/ppermute | solution.py:855
  284.8 3.5 all-to-all-start.4
  289.3 23.5 %all-to-all-done.4 = f32[8,16,768]{2,1,0:T(8,128)S(1)} async-done(((f32[8,16,768]{2,1,0:T(8,128)}), f32[8,16,768]{2,1,0:T(8,128)S(1)}, u32[]{:S(2)}, u32[]{:S(2)}) %all-to-all-start.4) | async-done | bytes 393248 | tf_op jit(solution)/shard_map/all_to_all | solution.py:842
  313.5 3.7 %all-to-all-start.5 = ((f32[4,16,768]{2,1,0:T(8,128)}), f32[4,16,768]{2,1,0:T(8,128)S(1)}, u32[]{:S(2)}, u32[]{:S(2)}) async-start(f32[4,16,768]{2,1,0:T(8,128)} %broadcast_in_dim.8), calls=%async_computation.7 | async-start | bytes 393216 | tf_op jit(solution)/shard_map/all_to_all | solution.py:842
  319.5 10.2 %all-to-all-done.5 = f32[4,16,768]{2,1,0:T(8,128)S(1)} async-done(((f32[4,16,768]{2,1,0:T(8,128)}), f32[4,16,768]{2,1,0:T(8,128)S(1)}, u32[]{:S(2)}, u32[]{:S(2)}) %all-to-all-start.5) | async-done | bytes 196640 | tf_op jit(solution)/shard_map/all_to_all | solution.py:842
  331.0 8.0 %finish.1 = (f32[768,768]{1,0:T(8,128)}, f32[768,2304]{1,0:T(8,128)}) custom-call(s32[8]{0:T(128)} %pad_add_fusion.where, bf16[96,3072]{1,0:T(8,128)(2,1)} %copy-done.4, bf16[96,3072]{1,0:T(8,128)(2,1)} %copy-done.7, bf16[96,3072]{1,0:T(8,128)(2,1)} %copy-done.8, bf16[96,3072]{1,0:T(8,128)(2,1)} %collective-permute-done.17.refs_3_, ...), custom_call_target="tpu_custom_call" | custom-call | flops 10000000 | bytes 100000 | tf_op jit(solution)/shard_map/finish/pallas_call | solution.py:797
  (134 shorter events, 38.7 us)
Async XLA Ops:
  12.7 44.4 %all-to-all-start = ((bf16[8,144,768]{2,1,0:T(8,128)(2,1)}), bf16[8,144,768]{2,1,0:T(8,128)(2,1)S(1)}, u32[]{:S(2)}, u32[]{:S(2)}) async-start(bf16[8,144,768]{2,1,0:T(8,128)(2,1)} %bitcast.44), calls=%async_computation | async-start | bytes 3538944 | tf_op jit(solution)/shard_map/all_to_all | solution.py:837
  58.4 27.3 %all-to-all-start.1 = ((bf16[8,144,768]{2,1,0:T(8,128)(2,1)}), bf16[8,144,768]{2,1,0:T(8,128)(2,1)S(1)}, u32[]{:S(2)}, u32[]{:S(2)}) async-start(bf16[8,144,768]{2,1,0:T(8,128)(2,1)} %bitcast.45), calls=%async_computation.1 | async-start | bytes 3538944 | tf_op jit(solution)/shard_map/all_to_all | solution.py:837
  62.5 142.1 %reduce-scatter.4.cloned.1.call-start = ((), (), s32[]{:S(2)}) async-start(), calls=%async_computation.9 | async-start | bytes 5898240 | tf_op jit(solution)/shard_map/reduce_scatter | solution.py:966
  126.3 26.8 %all-to-all-start.2 = ((bf16[8,144,768]{2,1,0:T(8,128)(2,1)}), bf16[8,144,768]{2,1,0:T(8,128)(2,1)S(1)}, u32[]{:S(2)}, u32[]{:S(2)}) async-start(bf16[8,144,768]{2,1,0:T(8,128)(2,1)} %bitcast.52), calls=%async_computation.2 | async-start | bytes 3538944 | tf_op jit(solution)/shard_map/all_to_all | solution.py:837
  154.3 41.7 %all-to-all-start.3 = ((bf16[8,144,768]{2,1,0:T(8,128)(2,1)}), bf16[8,144,768]{2,1,0:T(8,128)(2,1)S(1)}, u32[]{:S(2)}, u32[]{:S(2)}) async-start(bf16[8,144,768]{2,1,0:T(8,128)(2,1)} %bitcast.47), calls=%async_computation.3 | async-start | bytes 3538944 | tf_op jit(solution)/shard_map/all_to_all | solution.py:837
  157.9 91.4 %reduce-scatter.6.cloned.1.call-start = ((), (), s32[]{:S(2)}) async-start(), calls=%async_computation.10 | async-start | bytes 2949120 | tf_op jit(solution)/shard_map/reduce_scatter | solution.py:851
  158.7 180.4 %reduce-scatter.8.cloned.1.call-start = ((), (), s32[]{:S(2)}) async-start(), calls=%async_computation.11 | async-start | bytes 3072000 | tf_op jit(solution)/shard_map/reduce_scatter | solution.py:851
  196.0 3.8 %collective-permute-start.1 = (bf16[384,1536]{1,0:T(8,128)(2,1)}, bf16[384,1536]{1,0:T(8,128)(2,1)S(1)}, u32[]{:S(2)}, u32[]{:S(2)}) collective-permute-start(bf16[384,1536]{1,0:T(8,128)(2,1)} %get-tuple-element.104), channel_id=1, source_target_pairs={{0,1},{1,0},{2,3},{3,2},{4,5},{5,4},{6,7},{7,6},{8,9},{9,8},{10,11... | collective-permute-start | bytes 3538952 | tf_op jit(solution)/shard_map/ppermute | solution.py:855
  196.4 3.3 collective-permute-start
  217.7 3.9 %collective-permute-start.5 = (bf16[384,768]{1,0:T(8,128)(2,1)}, bf16[384,768]{1,0:T(8,128)(2,1)S(1)}, u32[]{:S(2)}, u32[]{:S(2)}) collective-permute-start(bf16[384,768]{1,0:T(8,128)(2,1)} %get-tuple-element.113), channel_id=1, source_target_pairs={{0,1},{1,0},{2,3},{3,2},{4,5},{5,4},{6,7},{7,6},{8,9},{9,8},{10,11... | collective-permute-start | bytes 1769480 | tf_op jit(solution)/shard_map/ppermute | solution.py:855
  218.2 14.1 %collective-permute-start.4 = (bf16[96,2304]{1,0:T(8,128)(2,1)}, bf16[96,2304]{1,0:T(8,128)(2,1)S(1)}, u32[]{:S(2)}, u32[]{:S(2)}) collective-permute-start(bf16[96,2304]{1,0:T(8,128)(2,1)} %get-tuple-element.108), channel_id=1, source_target_pairs={{0,6},{1,7},{2,4},{3,5},{4,2},{5,3},{6,0},{7,1},{8,14},{9,15},{10,... | collective-permute-start | bytes 1327112 | tf_op jit(solution)/shard_map/ppermute | solution.py:855
  220.8 21.0 %collective-permute-start.3 = (bf16[96,2304]{1,0:T(8,128)(2,1)S(1)}, bf16[96,2304]{1,0:T(8,128)(2,1)S(1)}, u32[]{:S(2)}, u32[]{:S(2)}) collective-permute-start(bf16[96,2304]{1,0:T(8,128)(2,1)S(1)} %copy-done.25), channel_id=1, source_target_pairs={{0,4},{1,5},{2,6},{3,7},{4,0},{5,1},{6,2},{7,3},{8,12},{9,13},{10,... | collective-permute-start | bytes 1327112 | tf_op jit(solution)/shard_map/ppermute | solution.py:855
  221.3 20.7 %collective-permute-start.2 = (bf16[96,2304]{1,0:T(8,128)(2,1)S(1)}, bf16[96,2304]{1,0:T(8,128)(2,1)S(1)}, u32[]{:S(2)}, u32[]{:S(2)}) collective-permute-start(bf16[96,2304]{1,0:T(8,128)(2,1)S(1)} %copy-done.24), channel_id=1, source_target_pairs={{0,2},{1,3},{2,0},{3,1},{4,6},{5,7},{6,4},{7,5},{8,10},{9,11},{10,... | collective-permute-start | bytes 1327112 | tf_op jit(solution)/shard_map/ppermute | solution.py:855
  224.5 24.6 %collective-permute-start.8 = (bf16[96,768]{1,0:T(8,128)(2,1)}, bf16[96,768]{1,0:T(8,128)(2,1)S(1)}, u32[]{:S(2)}, u32[]{:S(2)}) collective-permute-start(bf16[96,768]{1,0:T(8,128)(2,1)} %get-tuple-element.117), channel_id=1, source_target_pairs={{0,6},{1,7},{2,4},{3,5},{4,2},{5,3},{6,0},{7,1},{8,14},{9,15},{10,... | collective-permute-start | bytes 442376 | tf_op jit(solution)/shard_map/ppermute | solution.py:855
  227.2 22.0 %collective-permute-start.7 = (bf16[96,768]{1,0:T(8,128)(2,1)}, bf16[96,768]{1,0:T(8,128)(2,1)S(1)}, u32[]{:S(2)}, u32[]{:S(2)}) collective-permute-start(bf16[96,768]{1,0:T(8,128)(2,1)} %get-tuple-element.116), channel_id=1, source_target_pairs={{0,4},{1,5},{2,6},{3,7},{4,0},{5,1},{6,2},{7,3},{8,12},{9,13},{10,... | collective-permute-start | bytes 442376 | tf_op jit(solution)/shard_map/ppermute | solution.py:855
  232.3 16.9 %collective-permute-start.6 = (bf16[96,768]{1,0:T(8,128)(2,1)}, bf16[96,768]{1,0:T(8,128)(2,1)S(1)}, u32[]{:S(2)}, u32[]{:S(2)}) collective-permute-start(bf16[96,768]{1,0:T(8,128)(2,1)} %get-tuple-element.115), channel_id=1, source_target_pairs={{0,2},{1,3},{2,0},{3,1},{4,6},{5,7},{6,4},{7,5},{8,10},{9,11},{10,... | collective-permute-start | bytes 442376 | tf_op jit(solution)/shard_map/ppermute | solution.py:855
  249.4 15.4 %collective-permute-start.11 = (bf16[24,3072]{1,0:T(8,128)(2,1)S(1)}, bf16[24,3072]{1,0:T(8,128)(2,1)S(1)}, u32[]{:S(2)}, u32[]{:S(2)}) collective-permute-start(bf16[24,3072]{1,0:T(8,128)(2,1)S(1)} %get-tuple-element.152), channel_id=1, source_target_pairs={{0,24},{8,16},{16,8},{24,0},{1,25},{9,17},{17,9},{25,1},{2,26},{10... | collective-permute-start | bytes 442376 | tf_op jit(solution)/shard_map/ppermute | solution.py:855
  253.4 12.1 %collective-permute-start.10 = (bf16[24,3072]{1,0:T(8,128)(2,1)S(1)}, bf16[24,3072]{1,0:T(8,128)(2,1)S(1)}, u32[]{:S(2)}, u32[]{:S(2)}) collective-permute-start(bf16[24,3072]{1,0:T(8,128)(2,1)S(1)} %get-tuple-element.153), channel_id=1, source_target_pairs={{0,16},{8,24},{16,0},{24,8},{1,17},{9,25},{17,1},{25,9},{2,18},{10... | collective-permute-start | bytes 442376 | tf_op jit(solution)/shard_map/ppermute | solution.py:855
  253.4 12.1 %collective-permute-start.9 = (bf16[24,3072]{1,0:T(8,128)(2,1)S(1)}, bf16[24,3072]{1,0:T(8,128)(2,1)S(1)}, u32[]{:S(2)}, u32[]{:S(2)}) collective-permute-start(bf16[24,3072]{1,0:T(8,128)(2,1)S(1)} %get-tuple-element.151), channel_id=1, source_target_pairs={{0,8},{8,0},{16,24},{24,16},{1,9},{9,1},{17,25},{25,17},{2,10},{10... | collective-permute-start | bytes 442376 | tf_op jit(solution)/shard_map/ppermute | solution.py:855
  265.5 8.7 %collective-permute-start.12 = (bf16[24,3072]{1,0:T(8,128)(2,1)S(1)}, bf16[24,3072]{1,0:T(8,128)(2,1)S(1)}, u32[]{:S(2)}, u32[]{:S(2)}) collective-permute-start(bf16[24,3072]{1,0:T(8,128)(2,1)S(1)} %fusion.2), channel_id=1, source_target_pairs={{0,24},{8,16},{16,8},{24,0},{1,25},{9,17},{17,9},{25,1},{2,26},{10... | collective-permute-start | bytes 442376 | tf_op jit(solution)/shard_map/ppermute | solution.py:855
  268.7 11.4 %collective-permute-start.13 = (bf16[24,3072]{1,0:T(8,128)(2,1)S(1)}, bf16[24,3072]{1,0:T(8,128)(2,1)S(1)}, u32[]{:S(2)}, u32[]{:S(2)}) collective-permute-start(bf16[24,3072]{1,0:T(8,128)(2,1)S(1)} %fusion.2), channel_id=1, source_target_pairs={{0,16},{8,24},{16,0},{24,8},{1,17},{9,25},{17,1},{25,9},{2,18},{10... | collective-permute-start | bytes 442376 | tf_op jit(solution)/shard_map/ppermute | solution.py:855
  268.7 11.4 %collective-permute-start.14 = (bf16[24,3072]{1,0:T(8,128)(2,1)S(1)}, bf16[24,3072]{1,0:T(8,128)(2,1)S(1)}, u32[]{:S(2)}, u32[]{:S(2)}) collective-permute-start(bf16[24,3072]{1,0:T(8,128)(2,1)S(1)} %fusion.2), channel_id=1, source_target_pairs={{0,8},{8,0},{16,24},{24,16},{1,9},{9,1},{17,25},{25,17},{2,10},{10... | collective-permute-start | bytes 442376 | tf_op jit(solution)/shard_map/ppermute | solution.py:855
  280.3 37.6 %copy-start.5 = (bf16[768,768]{1,0:T(8,128)(2,1)S(1)}, bf16[768,768]{1,0:T(8,128)(2,1)}, u32[]{:S(2)}) copy-start(bf16[768,768]{1,0:T(8,128)(2,1)} %reduce-scatter.4.cloned.1.call-done) | copy-start | bytes 3538948
  280.3 36.9 %collective-permute-start.15 = (bf16[96,3072]{1,0:T(8,128)(2,1)S(1)}, bf16[96,3072]{1,0:T(8,128)(2,1)S(1)}, u32[]{:S(2)}, u32[]{:S(2)}) collective-permute-start(bf16[96,3072]{1,0:T(8,128)(2,1)S(1)} %pad_maximum_fusion.refs_0_), channel_id=1, source_target_pairs={{0,2},{1,3},{2,0},{3,1},{4,6},{5,7},{6,4},{7,5},{8,10},{9,11},{10,... | collective-permute-start | bytes 1769480 | tf_op jit(solution)/shard_map/ppermute | solution.py:855
  282.2 35.1 %collective-permute-start.16 = (bf16[96,3072]{1,0:T(8,128)(2,1)S(1)}, bf16[96,3072]{1,0:T(8,128)(2,1)S(1)}, u32[]{:S(2)}, u32[]{:S(2)}) collective-permute-start(bf16[96,3072]{1,0:T(8,128)(2,1)S(1)} %pad_maximum_fusion.refs_0_), channel_id=1, source_target_pairs={{0,4},{1,5},{2,6},{3,7},{4,0},{5,1},{6,2},{7,3},{8,12},{9,13},{10,... | collective-permute-start | bytes 1769480 | tf_op jit(solution)/shard_map/ppermute | solution.py:855
  282.3 35.5 %collective-permute-start.17 = (bf16[96,3072]{1,0:T(8,128)(2,1)S(1)}, bf16[96,3072]{1,0:T(8,128)(2,1)}, u32[]{:S(2)}, u32[]{:S(2)}) collective-permute-start(bf16[96,3072]{1,0:T(8,128)(2,1)S(1)} %pad_maximum_fusion.refs_0_), channel_id=1, source_target_pairs={{0,6},{1,7},{2,4},{3,5},{4,2},{5,3},{6,0},{7,1},{8,14},{9,15},{10,... | collective-permute-start | bytes 1769480 | tf_op jit(solution)/shard_map/ppermute | solution.py:855
  284.8 28.0 %all-to-all-start.4 = ((f32[8,16,768]{2,1,0:T(8,128)}), f32[8,16,768]{2,1,0:T(8,128)S(1)}, u32[]{:S(2)}, u32[]{:S(2)}) async-start(f32[8,16,768]{2,1,0:T(8,128)} %broadcast_in_dim.7), calls=%async_computation.6 | async-start | bytes 786432 | tf_op jit(solution)/shard_map/all_to_all | solution.py:842
  288.9 42.1 %collective-permute-start.18 = (bf16[96,3072]{1,0:T(8,128)(2,1)S(1)}, bf16[96,3072]{1,0:T(8,128)(2,1)}, u32[]{:S(2)}, u32[]{:S(2)}) collective-permute-start(bf16[96,3072]{1,0:T(8,128)(2,1)S(1)} %pad_maximum_fusion.refs_0_), channel_id=1, source_target_pairs={{0,1},{1,0},{2,3},{3,2},{4,5},{5,4},{6,7},{7,6},{8,9},{9,8},{10,11... | collective-permute-start | bytes 1769480 | tf_op jit(solution)/shard_map/ppermute | solution.py:855
  313.5 16.2 %all-to-all-start.5 = ((f32[4,16,768]{2,1,0:T(8,128)}), f32[4,16,768]{2,1,0:T(8,128)S(1)}, u32[]{:S(2)}, u32[]{:S(2)}) async-start(f32[4,16,768]{2,1,0:T(8,128)} %broadcast_in_dim.8), calls=%async_computation.7 | async-start | bytes 393216 | tf_op jit(solution)/shard_map/all_to_all | solution.py:842
  317.2 13.8 %collective-permute-start.19 = (bf16[96,3072]{1,0:T(8,128)(2,1)S(1)}, bf16[96,3072]{1,0:T(8,128)(2,1)}, u32[]{:S(2)}, u32[]{:S(2)}) collective-permute-start(bf16[96,3072]{1,0:T(8,128)(2,1)S(1)} %collective-permute-done.15.refs_1_), channel_id=1, source_target_pairs={{0,1},{1,0},{2,3},{3,2},{4,5},{5,4},{6,7},{7,6},{8,9},{9,8},{10,11... | collective-permute-start | bytes 1769480 | tf_op jit(solution)/shard_map/ppermute | solution.py:855
  317.3 13.7 %collective-permute-start.20 = (bf16[96,3072]{1,0:T(8,128)(2,1)S(1)}, bf16[96,3072]{1,0:T(8,128)(2,1)}, u32[]{:S(2)}, u32[]{:S(2)}) collective-permute-start(bf16[96,3072]{1,0:T(8,128)(2,1)S(1)} %collective-permute-done.16.refs_2_), channel_id=1, source_target_pairs={{0,1},{1,0},{2,3},{3,2},{4,5},{5,4},{6,7},{7,6},{8,9},{9,8},{10,11... | collective-permute-start | bytes 1769480 | tf_op jit(solution)/shard_map/ppermute | solution.py:855
  317.8 13.2 %collective-permute-start.21 = (bf16[96,3072]{1,0:T(8,128)(2,1)}, bf16[96,3072]{1,0:T(8,128)(2,1)}, u32[]{:S(2)}, u32[]{:S(2)}) collective-permute-start(bf16[96,3072]{1,0:T(8,128)(2,1)} %collective-permute-done.17.refs_3_), channel_id=1, source_target_pairs={{0,1},{1,0},{2,3},{3,2},{4,5},{5,4},{6,7},{7,6},{8,9},{9,8},{10,11... | collective-permute-start | bytes 1769480 | tf_op jit(solution)/shard_map/ppermute | solution.py:855
  (25 other events, 181.8 us)
Sparse Core Ops, SparseCore 0:
  112.9 84.6 reduce-scatter.3
  200.5 48.5 reduce-scatter.5
  280.4 52.0 reduce-scatter.7
